TPU v7x, 32 devices: a whole 2x2x4 slice. The times are simulated.
32 devices in a mesh: tm: 8 (over z, x), tensor: 4 (over y, core).
Axes of the slice: x: 2, y: 2, z: 4, core: 2. Of those that a mesh axis runs over, the one named last changes fastest.
Arguments:
- frames: bfloat16 [8192, 3072], P('tm', 'tensor'), may hold values from -9 to 9
- w_query: bfloat16 [3072, 2048], P(None, 'tensor'), may hold values from -0.09111309 to 0.09111309
- w_key: bfloat16 [3072, 2048], P(None, 'tensor'), may hold values from -0.12719748 to 0.12719748
- w_value: bfloat16 [3072, 2048], P(None, 'tensor'), may hold values from -0.109375 to 0.109375
- w_out: bfloat16 [2048, 3072], P('tensor'), may hold values from -0.125 to 0.125
- head_gain: float32 [3072], P('tensor'), may hold values from 0.25 to 1.75
- reward_weight: float32 [3072, 255], P('tensor'), may hold values from -0.75 to 0.75
- term_weight: float32 [3072], P('tensor'), may hold values from -0.109375 to 0.109375
- out_grad: bfloat16 [8192, 3072], P('tm', 'tensor'), may hold values from -0.75 to 0.75
- reward_bins: int32 [16], P('tm'), may hold values from 0 to 254
- episode_flags: int32 [16], P('tm'), may hold values from 0 to 2
Outputs:
- mixed: bfloat16 [8192, 3072], P('tm', 'tensor')
- pair_losses: float32 [2, 16], P(None, 'tm')
- grad_query: float32 [3072, 2048], P('tm', 'tensor')
- grad_key: float32 [3072, 2048], P('tm', 'tensor')
- grad_value: float32 [3072, 2048], P('tm', 'tensor')
- grad_out: float32 [2048, 3072], P('tensor', 'tm')
- grad_reward: float32 [3072, 255], P('tensor')
- grad_term: float32 [3072], P('tensor')
- grad_gain: float32 [3072], P('tensor')
Inputs may be any that keep to these rules, and one draw needn't show every extreme that they name: `episode_flags`: 0: the episode goes on over the pair, 1: it terminates at the pair, 2: the pair straddles a reset and is left out.
All inputs are finite; a program needn't handle non-finite values.
Results may differ from a plain program's by a relative error of at most 0.024.
Values may be sent and summed in bfloat16 or wider, within the bound.
A program may use at most 128 MiB of HBM per device.

v0:
```python
import jax
import jax.numpy as jnp
from jax import lax
from jax.sharding import PartitionSpec as P

HD = 128
PATCHES = 512


def from_behind(x, axis, by):
    size = lax.axis_size(axis)
    pairs = [(i, i + by) for i in range(size) if 0 <= i + by < size]
    return lax.ppermute(x, axis, pairs)


def local(
    frames,
    w_query,
    w_key,
    w_value,
    w_out,
    head_gain,
    reward_weight,
    term_weight,
    out_grad,
    reward_bins,
    episode_flags,
):
    f32 = jnp.float32
    bf16 = jnp.bfloat16
    highest = lax.Precision.HIGHEST
    rows, local_width = frames.shape
    span = PATCHES
    pairs = rows // span
    width = w_query.shape[1]
    heads_here = width // HD
    full_width = w_out.shape[1]
    scale_qk = HD ** (-0.5)
    tm_count = lax.axis_size("tm")
    position = lax.axis_index("tm")
    is_last = position == tm_count - 1
    frame_total = tm_count * pairs
    gathered = lax.all_gather(frames, "tensor", axis=1, tiled=True)
    query_part = jnp.dot(gathered, w_query, preferred_element_type=f32)
    key_part = jnp.dot(gathered, w_key, preferred_element_type=f32)
    value_part = jnp.dot(gathered, w_value, preferred_element_type=f32)
    queries = query_part.astype(bf16)
    keys = key_part.astype(bf16)
    values = value_part.astype(bf16)
    next_keys, next_values = from_behind((keys[:span], values[:span]), "tm", -1)
    keys = jnp.concatenate([keys, next_keys], 0)
    values = jnp.concatenate([values, next_values], 0)
    query_blocks = queries.reshape(pairs, span, heads_here, HD)
    key_blocks = jnp.stack(
        [keys[index * span : (index + 2) * span] for index in range(pairs)]
    ).reshape(pairs, 2 * span, heads_here, HD)
    value_blocks = jnp.stack(
        [values[index * span : (index + 2) * span] for index in range(pairs)]
    ).reshape(pairs, 2 * span, heads_here, HD)
    key_index = jnp.arange(2 * span, dtype=jnp.int32)
    pair_index = jnp.arange(pairs, dtype=jnp.int32)
    cut = (is_last & (pair_index == pairs - 1))[:, None] & (key_index >= span)[None, :]
    scores = (
        jnp.einsum("fqhd,fkhd->fhqk", query_blocks, key_blocks, preferred_element_type=f32)
        * scale_qk
    )
    scores = jnp.where(cut[:, None, None, :], -1e30, scores)
    probs = jax.nn.softmax(scores, axis=-1)
    weights = probs.astype(bf16)
    attended = (
        jnp.einsum("fhqk,fkhd->fqhd", weights, value_blocks, preferred_element_type=f32)
        .astype(bf16)
        .reshape(rows, width)
    )
    partial_out = jnp.dot(attended, w_out, preferred_element_type=f32)
    summed = lax.psum_scatter(
        partial_out.astype(jnp.bfloat16), "tensor", scatter_dimension=1, tiled=True
    ).astype(jnp.float32)
    mixed = (frames.astype(f32) + summed).astype(bf16)
    pooled = mixed.astype(f32).reshape(pairs, span, local_width).mean(axis=1)
    gained = pooled * head_gain[None, :]
    square_part = jnp.sum(pooled * pooled, axis=-1)
    raw_reward = jnp.dot(gained, reward_weight, precision=highest)
    raw_term = jnp.dot(gained, term_weight, precision=highest)
    squares = lax.psum(square_part, "tensor")
    scale = lax.rsqrt(squares / full_width + 1e-05)
    reward_logits, term_logit = lax.psum((scale[:, None] * raw_reward, scale * raw_term), "tensor")
    frame_ids = position * pairs + pair_index
    live = ((episode_flags != 2) & (frame_ids < frame_total - 1)).astype(f32)
    target = (episode_flags == 1).astype(f32)
    bins_count = reward_weight.shape[1]
    onehot = (reward_bins[:, None] == jnp.arange(bins_count, dtype=jnp.int32)[None, :]).astype(f32)
    reward_loss = live * (
        jax.scipy.special.logsumexp(reward_logits, axis=-1)
        - jnp.sum(onehot * reward_logits, axis=-1)
    )
    term_loss = live * (jax.nn.softplus(term_logit) - target * term_logit)
    pair_losses = jnp.stack([reward_loss, term_loss])
    logit_grad = live[:, None] * (jax.nn.softmax(reward_logits, axis=-1) - onehot)
    term_grad = live * (jax.nn.sigmoid(term_logit) - target)
    scale_grad = (jnp.sum(logit_grad * reward_logits, axis=-1) + term_grad * term_logit) / scale
    gain_input_grad = scale[:, None] * (
        jnp.dot(logit_grad, reward_weight.T, precision=highest)
        + term_grad[:, None] * term_weight[None, :]
    )
    pooled_grad = (
        head_gain[None, :] * gain_input_grad
        - (scale_grad * scale**3)[:, None] * pooled / full_width
    )
    reward_part = jnp.dot(gained.T, scale[:, None] * logit_grad, precision=highest)
    term_part = jnp.dot(gained.T, scale * term_grad, precision=highest)
    gain_part = jnp.sum(pooled * gain_input_grad, axis=0)
    grad_reward, grad_term, grad_gain = (
        lax.psum(reward_part.astype(jnp.bfloat16), "tm").astype(jnp.float32),
        lax.psum(term_part.astype(jnp.bfloat16), "tm").astype(jnp.float32),
        lax.psum(gain_part.astype(jnp.bfloat16), "tm").astype(jnp.float32),
    )
    mixed_grad = (
        (out_grad.astype(f32).reshape(pairs, span, local_width) + pooled_grad[:, None, :] / span)
        .reshape(rows, local_width)
        .astype(bf16)
    )
    piece = lax.all_gather(mixed_grad, "tensor", axis=1, tiled=True)
    attended_sum = lax.dot_general(
        piece, w_out, (((1,), (1,)), ((), ())), preferred_element_type=f32
    )
    block = lax.dot_general(attended, piece, (((0,), (0,)), ((), ())), preferred_element_type=f32)
    attended_sum, out_weight_grad = (attended_sum, block)
    attended_grad = attended_sum.astype(bf16).reshape(pairs, span, heads_here, HD)
    prob_grad = jnp.einsum(
        "fqhd,fkhd->fhqk", attended_grad, value_blocks, preferred_element_type=f32
    )
    value_pair = (
        jnp.einsum("fhqk,fqhd->fkhd", weights, attended_grad, preferred_element_type=f32)
        .astype(bf16)
        .reshape(pairs, 2 * span, width)
    )
    delta = jnp.sum(prob_grad * probs, axis=-1, keepdims=True)
    score_grad = (probs * (prob_grad - delta) * scale_qk).astype(bf16)
    query_grad = (
        jnp.einsum("fhqk,fkhd->fqhd", score_grad, key_blocks, preferred_element_type=f32)
        .astype(bf16)
        .reshape(rows, width)
    )
    key_pair = (
        jnp.einsum("fhqk,fqhd->fkhd", score_grad, query_blocks, preferred_element_type=f32)
        .astype(bf16)
        .reshape(pairs, 2 * span, width)
    )
    grad_pieces = [(0, key_pair[0], value_pair[0])]
    grad_pieces.append(
        ((pairs - 1) * span, key_pair[pairs - 1][:span], value_pair[pairs - 1][:span])
    )
    returned_key, returned_value = from_behind(
        (key_pair[pairs - 1][span:], value_pair[pairs - 1][span:]), "tm", 1
    )
    grad_pieces.append((0, returned_key, returned_value))

    def contract(left, right):
        return lax.dot_general(left, right, (((0,), (0,)), ((), ())), preferred_element_type=f32)

    grad_q = contract(gathered, query_grad)
    grad_k = jnp.zeros((gathered.shape[1], width), f32)
    grad_v = jnp.zeros((gathered.shape[1], width), f32)
    for first_row, key_rows, value_rows in grad_pieces:
        feats = gathered[first_row : first_row + key_rows.shape[0]]
        grad_k = grad_k + contract(feats, key_rows)
        grad_v = grad_v + contract(feats, value_rows)
    stacked = jnp.concatenate([grad_q, grad_k, grad_v], 1)
    grad_query, grad_key, grad_value = (
        lax.psum_scatter(
            stacked[:, :width].astype(jnp.bfloat16), "tm", scatter_dimension=0, tiled=True
        ).astype(jnp.float32),
        lax.psum_scatter(
            stacked[:, width : 2 * width].astype(jnp.bfloat16),
            "tm",
            scatter_dimension=0,
            tiled=True,
        ).astype(jnp.float32),
        lax.psum_scatter(
            stacked[:, 2 * width :].astype(jnp.bfloat16), "tm", scatter_dimension=0, tiled=True
        ).astype(jnp.float32),
    )
    grad_out = lax.psum_scatter(
        out_weight_grad.astype(jnp.bfloat16), "tm", scatter_dimension=1, tiled=True
    ).astype(jnp.float32)
    return (
        mixed,
        pair_losses,
        grad_query,
        grad_key,
        grad_value,
        grad_out,
        grad_reward,
        grad_term,
        grad_gain,
    )


def solution(mesh):
    return jax.shard_map(
        local,
        mesh=mesh,
        in_specs=(
            P("tm", "tensor"),
            P(None, "tensor"),
            P(None, "tensor"),
            P(None, "tensor"),
            P("tensor", None),
            P("tensor"),
            P("tensor", None),
            P("tensor"),
            P("tm", "tensor"),
            P("tm"),
            P("tm"),
        ),
        out_specs=(
            P("tm", "tensor"),
            P(None, "tm"),
            P("tm", "tensor"),
            P("tm", "tensor"),
            P("tm", "tensor"),
            P("tensor", "tm"),
            P("tensor", None),
            P("tensor"),
            P("tensor"),
        ),
        check_vma=False,
    )
```

profile of v0, /device:TPU:0, one launch (start us, length us, event | category | flops | bytes accessed | tf_op | source)
XLA Modules:
  0.0 668.2 jit_solution(4629825863376091513)
XLA Ops:
  8.1 50.6 %all-gather.3.cloned.1.call-done = bf16[1024,3072]{1,0:T(8,128)(2,1)} async-done(((bf16[1024,768]{1,0:T(8,128)(2,1)}), bf16[1024,3072]{1,0:T(8,128)(2,1)}) %all-gather.3.cloned.1.call-update) | async-done | bytes 6291472 | tf_op jit(solution)/shard_map/all_gather | solution.py:43
  58.7 7.3 %convolution_convert_fusion.4 = bf16[1024,512]{0,1:T(8,128)(2,1)S(1)} fusion(bf16[1024,3072]{1,0:T(8,128)(2,1)} %all-gather.3.cloned.1.call-done, bf16[3072,512]{1,0:T(8,128)(2,1)} %param.13), kind=kOutput, calls=%fused_computation.43 | convolution fusion | flops 3221749760 | bytes 10485760 | tf_op jit(solution)/shard_map/dot_general | solution.py:45
  68.2 3.4 convolution_convert_fusion.6
  75.0 2.3 copy.44
  77.3 8.1 %convolution_convert_fusion.5 = bf16[1024,512]{1,0:T(8,128)(2,1)} fusion(bf16[1024,3072]{1,0:T(8,128)(2,1)} %all-gather.3.cloned.1.call-done, bf16[3072,512]{1,0:T(8,128)(2,1)} %param.12), kind=kOutput, calls=%fused_computation.44 | convolution fusion | flops 3221749760 | bytes 10485760 | tf_op jit(solution)/shard_map/dot_general | solution.py:44
  85.4 2.1 reshape.113
  87.5 2.4 copy.52
  89.9 2.3 pad_maximum_fusion.4
  92.2 2.2 copy.45
  94.4 10.6 %fusion.87 = (f32[2,4,512]{2,1,0:T(4,128)S(1)}, f32[2,4,512,1024]{3,2,1,0:T(8,128)}) fusion(pred[2,1024]{1,0:T(4,128)(4,1)S(1)} %broadcast_and_fusion, bf16[2,512,4,128]{1,3,2,0:T(8,128)(2,1)} %copy.52, bf16[1,1024,4,128]{3,1,2,0:T(8,128)(2,1)} %copy.45, bf16[1,1024,4,128]{3,1,2,0:T(8,128)(2,1)} %copy.44), kind=kOutput, calls=%fused_computation.116 | convolution fusion | flops 1091568640 | bytes 19941376 | tf_op jit(solution)/shard_map/sub | solution.py:68
  107.4 8.5 %fusion.44 = bf16[2,512,4,128]{1,3,2,0:T(8,128)(2,1)} fusion(bf16[1,1024,4,128]{1,3,2,0:T(8,128)(2,1)S(1)} %bitcast.97, bf16[1,1024,4,128]{1,3,2,0:T(8,128)(2,1)} %bitcast.94, f32[2,4,512,1024]{3,2,1,0:T(8,128)} %get-tuple-element.56, f32[2,4,512]{2,1,0:T(4,128)S(1)} %get-tuple-element.55), kind=kOutput, calls=%fused_computation.48 | convolution fusion | flops 1083703296 | bytes 19939328 | tf_op jit(solution)/shard_map/fhqk,fkhd->fqhd/dot_general | solution.py:71
  115.9 2.4 copy.47
  118.3 6.6 convolution_convert_fusion
  125.7 61.9 %reduce-scatter.14.cloned.1.call-done = bf16[1024,768]{1,0:T(8,128)(2,1)} async-done(((bf16[1024,3072]{1,0:T(8,128)(2,1)}), bf16[1024,768]{1,0:T(8,128)(2,1)}) %reduce-scatter.14.cloned.1.call-update) | async-done | bytes 1572880 | tf_op jit(solution)/shard_map/reduce_scatter | solution.py:76
  187.6 3.5 convert_reduce_fusion
  191.2 5.8 psum.42
  197.1 1.6 convolution_multiply_fusion
  198.7 5.7 all-reduce
  204.9 1.9 multiply_reduce_fusion.1
  206.8 2.8 fusion.22
  209.8 1.6 convolution_convert_fusion.7
  211.4 46.2 %all-gather.5.cloned.1.call-done = bf16[1024,3072]{1,0:T(8,128)(2,1)} async-done(((bf16[1024,768]{1,0:T(8,128)(2,1)}), bf16[1024,3072]{1,0:T(8,128)(2,1)}) %all-gather.5.cloned.1.call-update) | async-done | bytes 6291472 | tf_op jit(solution)/shard_map/all_gather | solution.py:123
  257.6 8.3 %convolution_convert_fusion.1 = bf16[512,3072]{1,0:T(8,128)(2,1)} fusion(bf16[1024,3072]{1,0:T(8,128)(2,1)} %all-gather.5.cloned.1.call-done, bf16[128,8,4,128]{3,2,1,0:T(4,128)(2,1)} %bitcast.103), kind=kOutput, calls=%fused_computation.17 | convolution fusion | flops 3222798336 | bytes 10485760 | tf_op jit(solution)/shard_map/dot_general | solution.py:127
  265.9 4.7 copy.65
  271.1 7.3 %convolution_convert_fusion.3 = bf16[1024,512]{1,0:T(8,128)(2,1)} fusion(bf16[1024,3072]{1,0:T(8,128)(2,1)} %all-gather.5.cloned.1.call-done, bf16[512,3072]{1,0:T(8,128)(2,1)S(1)} %copy-done), kind=kOutput, calls=%fused_computation.42 | convolution fusion | flops 3221749760 | bytes 10485760 | tf_op jit(solution)/shard_map/dot_general | solution.py:124
  280.4 9.8 %fusion.47 = f32[2,4,512,1024]{3,2,1,0:T(8,128)} fusion(bf16[2,512,4,128]{1,3,2,0:T(8,128)(2,1)S(1)} %copy.53, bf16[1,1024,4,128]{1,3,2,0:T(8,128)(2,1)} %bitcast.98, bf16[1,1024,4,128]{1,3,2,0:T(8,128)(2,1)} %bitcast.95), kind=kOutput, calls=%fused_computation.49 | convolution fusion | flops 1074790400 | bytes 19922944 | tf_op jit(solution)/shard_map/fqhd,fkhd->fhqk/dot_general | solution.py:130
  290.2 32.6 %fusion.41 = bf16[2,512,4,128]{1,3,2,0:T(8,128)(2,1)} fusion(f32[2,4,512,1024]{3,2,1,0:T(8,128)} %fusion.47, bf16[1,1024,4,128]{3,1,2,0:T(8,128)(2,1)S(1)} %copy-done.7, bf16[1,1024,4,128]{3,1,2,0:T(8,128)(2,1)S(1)} %copy-done.6, f32[2,4,512,1024]{3,2,1,0:T(8,128)} %get-tuple-element.56, f32[2,4,512]{2,1,0:T(4,128)S(1)} %get-tuple-element.55), kind=kOutput, calls=%fused_computation.47 | convolution fusion | flops 1104679936 | bytes 36716544 | tf_op jit(solution)/shard_map/fhqk,fkhd->fqhd/dot_general | solution.py:141
  322.7 1.7 copy.51
  324.4 7.7 %fusion.19 = bf16[3072,512]{0,1:T(8,128)(2,1)} fusion(bf16[1024,3072]{1,0:T(8,128)(2,1)} %all-gather.3.cloned.1.call-done, bf16[128,8,4,128]{3,2,1,0:T(4,128)(2,1)S(1)} %bitcast.106), kind=kOutput, calls=%fused_computation.23 | convolution fusion | flops 3222798336 | bytes 10485760 | tf_op jit(solution)/shard_map/dot_general | solution.py:160
  332.1 4.7 copy.59
  336.8 7.1 %convert_bitcast_fusion = bf16[2,1024,4,128]{1,3,2,0:T(8,128)(2,1)S(1)} fusion(bf16[2,512,4,128]{1,3,2,0:T(8,128)(2,1)S(1)} %copy.53, f32[2,4,512,1024]{3,2,1,0:T(8,128)} %get-tuple-element.56, f32[2,4,512]{2,1,0:T(4,128)S(1)} %get-tuple-element.55), kind=kOutput, calls=%fused_computation.38 | convolution fusion | flops 1083179008 | bytes 19939328 | tf_op jit(solution)/shard_map/fhqk,fqhd->fkhd/dot_general | solution.py:134
  344.2 3.6 collective-permute-start.3
  347.8 5.7 fusion.89
  353.5 3.7 fusion.25
  357.2 5.4 collective-permute-done.3
  362.6 1.8 fusion.21
  364.5 2.9 copy.63
  367.4 29.7 %convert_bitcast_fusion.1 = bf16[2,1024,4,128]{1,3,2,0:T(8,128)(2,1)S(1)} fusion(bf16[2,512,4,128]{1,3,2,0:T(8,128)(2,1)} %copy.52, f32[2,4,512,1024]{3,2,1,0:T(8,128)} %fusion.47, f32[2,4,512,1024]{3,2,1,0:T(8,128)} %get-tuple-element.56, f32[2,4,512]{2,1,0:T(4,128)S(1)} %get-tuple-element.55), kind=kOutput, calls=%fused_computation.39 | convolution fusion | flops 1104155648 | bytes 36716544 | tf_op jit(solution)/shard_map/fhqk,fqhd->fkhd/dot_general | solution.py:146
  397.3 11.5 %collective-permute-start.2 = (bf16[512,512]{0,1:T(8,128)(2,1)S(1)}, bf16[512,512]{0,1:T(8,128)(2,1)S(1)}, u32[]{:S(2)}, u32[]{:S(2)}) collective-permute-start(bf16[512,512]{0,1:T(8,128)(2,1)S(1)} %bitcast.108), channel_id=1, source_target_pairs={{0,4},{4,8},{8,12},{12,16},{16,20},{20,24},{24,28},{1,5},{5,9},{9,... | collective-permute-start | bytes 1572872 | tf_op jit(solution)/shard_map/ppermute | solution.py:13
  408.8 5.7 fusion.88
  414.5 3.7 fusion.27
  419.7 3.5 fusion.20
  423.2 4.8 copy.61
  428.2 29.2 %all-reduce.1 = (bf16[768]{0:T(1024)(128)(2,1)S(1)}, bf16[768]{0:T(1024)(128)(2,1)S(1)}) all-reduce(bf16[768]{0:T(1024)(128)(2,1)S(1)} %convolution_reduce_fusion, bf16[768]{0:T(1024)(128)(2,1)S(1)} %get-tuple-element.51), channel_id=1, replica_groups=mesh['tm'=8,'tensor'=4] {'tm'}, use_global_device_ids=true, to_apply=%region_19.20 | all-reduce | flops 1536 | bytes 6144 | tf_op jit(solution)/shard_map/psum | solution.py:115
  459.2 1.9 convert_element_type.156
  463.3 41.2 %reduce-scatter.16.cloned.1.call-done = bf16[384,512]{1,0:T(8,128)(2,1)} async-done(((bf16[3072,512]{1,0:T(8,128)(2,1)}), bf16[384,512]{1,0:T(8,128)(2,1)}) %reduce-scatter.16.cloned.1.call-update) | async-done | bytes 393232
  506.8 74.9 %reduce-scatter.20.cloned.1.call-done = bf16[384,512]{1,0:T(8,128)(2,1)} async-done(((bf16[3072,512]{1,0:T(8,128)(2,1)}), bf16[384,512]{1,0:T(8,128)(2,1)}) %reduce-scatter.20.cloned.1.call-update) | async-done | bytes 393232
  584.0 74.9 %reduce-scatter.18.cloned.1.call-done = bf16[384,512]{1,0:T(8,128)(2,1)} async-done(((bf16[3072,512]{1,0:T(8,128)(2,1)}), bf16[384,512]{1,0:T(8,128)(2,1)}) %reduce-scatter.18.cloned.1.call-update) | async-done | bytes 393232
  (94 shorter events, 25.6 us)
Async XLA Ops:
  7.2 111.2 %copy-start = (bf16[512,3072]{1,0:T(8,128)(2,1)S(1)}, bf16[512,3072]{1,0:T(8,128)(2,1)}, u32[]{:S(2)}) copy-start(bf16[512,3072]{1,0:T(8,128)(2,1)} %param.15) | copy-start | bytes 9437188
  7.2 51.5 %all-gather.3.cloned.1.call-start = ((), (), s32[]{:S(2)}) async-start(), calls=%async_computation.5 | async-start | bytes 7864320 | tf_op jit(solution)/shard_map/all_gather | solution.py:43
  7.9 179.6 %reduce-scatter.14.cloned.1.call-start = ((), (), s32[]{:S(2)}) async-start(), calls=%async_computation.6 | async-start | bytes 7864320 | tf_op jit(solution)/shard_map/reduce_scatter | solution.py:76
  58.7 9.5 %copy-start.2 = (bf16[1024,3072]{1,0:T(8,128)(2,1)S(1)}, bf16[1024,3072]{1,0:T(8,128)(2,1)}, u32[]{:S(2)}) copy-start(bf16[1024,3072]{1,0:T(8,128)(2,1)} %all-gather.3.cloned.1.call-done) | copy-start | bytes 18874372
  58.7 9.5 %copy-start.12 = (bf16[3072,512]{1,0:T(8,128)(2,1)S(1)}, bf16[3072,512]{1,0:T(8,128)(2,1)}, u32[]{:S(2)}) copy-start(bf16[3072,512]{1,0:T(8,128)(2,1)} %param.14) | copy-start | bytes 9437188
  66.0 5.7 copy-start.4
  66.9 23.0 %collective-permute-start.1 = (bf16[512,512]{0,1:T(8,128)(2,1)}, bf16[512,512]{0,1:T(8,128)(2,1)}, u32[]{:S(2)}, u32[]{:S(2)}) collective-permute-start(bf16[512,512]{0,1:T(8,128)(2,1)} %slice.77), channel_id=1, source_target_pairs={{4,0},{8,4},{12,8},{16,12},{20,16},{24,20},{28,24},{5,1},{9,5},{13... | collective-permute-start | bytes 1572872 | tf_op jit(solution)/shard_map/ppermute | solution.py:13
  71.7 1.0 copy-start.3
  73.6 31.5 %collective-permute-start = (bf16[512,512]{0,1:T(8,128)(2,1)}, bf16[512,512]{0,1:T(8,128)(2,1)}, u32[]{:S(2)}, u32[]{:S(2)}) collective-permute-start(bf16[512,512]{0,1:T(8,128)(2,1)} %slice.76), channel_id=1, source_target_pairs={{4,0},{8,4},{12,8},{16,12},{20,16},{24,20},{28,24},{5,1},{9,5},{13... | collective-permute-start | bytes 1572872 | tf_op jit(solution)/shard_map/ppermute | solution.py:13
  106.4 1.0 copy-start.5
  125.0 0.7 copy-start.9
  125.0 66.2 %copy-start.8 = (f32[768]{0:T(1024)S(1)}, f32[768]{0:T(1024)}, u32[]{:S(2)}) copy-start(f32[768]{0:T(1024)} %param.18) | copy-start | bytes 9220
  125.0 73.7 %copy-start.11 = (s32[2]{0:T(128)S(1)}, s32[2]{0:T(128)}, u32[]{:S(2)}) copy-start(s32[2]{0:T(128)} %param.21) | copy-start | bytes 28
  125.0 79.7 %copy-start.10 = (s32[2]{0:T(128)S(1)}, s32[2]{0:T(128)}, u32[]{:S(2)}) copy-start(s32[2]{0:T(128)} %param.20) | copy-start | bytes 28
  125.0 132.6 %all-gather.5.cloned.1.call-start = ((), (), s32[]{:S(2)}) async-start(), calls=%async_computation.7 | async-start | bytes 7864320 | tf_op jit(solution)/shard_map/all_gather | solution.py:123
  209.7 249.5 %all-reduce.4.cloned.1.call-start = ((), (), s32[]{:S(2)}) async-start(), calls=%async_computation.8 | async-start | bytes 786432 | tf_op jit(solution)/shard_map/psum | solution.py:114
  211.4 249.8 %reduce-scatter.22.cloned.1.call-start = ((), (), s32[]{:S(2)}) async-start(), calls=%async_computation.12 | async-start | bytes 3538944
  270.6 233.9 %reduce-scatter.16.cloned.1.call-start = ((), (), s32[]{:S(2)}) async-start(), calls=%async_computation.9 | async-start | bytes 3538944
  280.4 9.8 %copy-start.6 = (bf16[1,1024,4,128]{3,1,2,0:T(8,128)(2,1)S(1)}, bf16[1,1024,4,128]{3,1,2,0:T(8,128)(2,1)}, u32[]{:S(2)}) copy-start(bf16[1,1024,4,128]{3,1,2,0:T(8,128)(2,1)} %copy.44) | copy-start | bytes 3145732
  280.4 9.8 %copy-start.7 = (bf16[1,1024,4,128]{3,1,2,0:T(8,128)(2,1)S(1)}, bf16[1,1024,4,128]{3,1,2,0:T(8,128)(2,1)}, u32[]{:S(2)}) copy-start(bf16[1,1024,4,128]{3,1,2,0:T(8,128)(2,1)} %copy.45) | copy-start | bytes 3145732
  336.8 244.9 %reduce-scatter.20.cloned.1.call-start = ((), (), s32[]{:S(2)}) async-start(), calls=%async_computation.11 | async-start | bytes 3538944
  344.2 18.5 %collective-permute-start.3 = (bf16[512,512]{0,1:T(8,128)(2,1)S(1)}, bf16[512,512]{0,1:T(8,128)(2,1)S(1)}, u32[]{:S(2)}, u32[]{:S(2)}) collective-permute-start(bf16[512,512]{0,1:T(8,128)(2,1)S(1)} %bitcast.107), channel_id=1, source_target_pairs={{0,4},{4,8},{8,12},{12,16},{16,20},{20,24},{24,28},{1,5},{5,9},{9,... | collective-permute-start | bytes 1572872 | tf_op jit(solution)/shard_map/ppermute | solution.py:13
  347.8 14.9 %slice-start = ((s8[6291456]{0:T(1024)(128)(4,1)}), s8[4194304]{0:T(1024)(128)(4,1)S(1)}, s32[]{:S(2)}) async-start(s8[6291456]{0:T(1024)(128)(4,1)} %bitcast.89), calls=%async_computation.13 | async-start | bytes 8388608
  347.8 14.9 %slice-start.1 = ((s8[6291456]{0:T(1024)(128)(4,1)}), s8[2097152]{0:T(1024)(128)(4,1)S(1)}, s32[]{:S(2)}) async-start(s8[6291456]{0:T(1024)(128)(4,1)} %bitcast.89), calls=%async_computation.14 | async-start | bytes 4194304
  367.4 291.6 %reduce-scatter.18.cloned.1.call-start = ((), (), s32[]{:S(2)}) async-start(), calls=%async_computation.10 | async-start | bytes 3538944
  397.3 22.4 %collective-permute-start.2 = (bf16[512,512]{0,1:T(8,128)(2,1)S(1)}, bf16[512,512]{0,1:T(8,128)(2,1)S(1)}, u32[]{:S(2)}, u32[]{:S(2)}) collective-permute-start(bf16[512,512]{0,1:T(8,128)(2,1)S(1)} %bitcast.108), channel_id=1, source_target_pairs={{0,4},{4,8},{8,12},{12,16},{16,20},{20,24},{24,28},{1,5},{5,9},{9,... | collective-permute-start | bytes 1572872 | tf_op jit(solution)/shard_map/ppermute | solution.py:13
  408.8 10.9 %slice-start.2 = ((s8[6291456]{0:T(1024)(128)(4,1)}), s8[4194304]{0:T(1024)(128)(4,1)S(1)}, s32[]{:S(2)}) async-start(s8[6291456]{0:T(1024)(128)(4,1)} %bitcast.91), calls=%async_computation.15 | async-start | bytes 8388608
  408.8 10.9 %slice-start.3 = ((s8[6291456]{0:T(1024)(128)(4,1)}), s8[2097152]{0:T(1024)(128)(4,1)S(1)}, s32[]{:S(2)}) async-start(s8[6291456]{0:T(1024)(128)(4,1)} %bitcast.91), calls=%async_computation.16 | async-start | bytes 4194304
  423.2 238.0 %copy-start.1 = (bf16[512,3072]{1,0:T(8,128)(2,1)S(1)}, bf16[512,3072]{1,0:T(8,128)(2,1)}, u32[]{:S(2)}) copy-start(bf16[512,3072]{1,0:T(8,128)(2,1)} %param.15) | copy-start | bytes 9437188
Sparse Core Ops, SparseCore 0:
  9.6 49.0 all-gather.2
  125.1 62.3 reduce-scatter.13
  209.8 47.7 all-gather.4
  261.7 71.2 all-reduce.3
  336.5 84.6 reduce-scatter.21
  424.6 79.8 reduce-scatter.15
  508.1 73.5 reduce-scatter.19
  585.3 73.5 reduce-scatter.17
where the time goes:
time: 675 us; the launch traced here: 668 us
  waiting for transfers between devices  357 us (53%)
  matrix products  177 us (26%)
  local copies, waits for them, and re-layouts  44.9 us (7%)
  blocking collectives  40.6 us (6%)
  starting transfers between devices  18.6 us (3%)
  other arithmetic  15.3 us (2%)
  between operations  14.7 us (2%)
    unnamed x12, waiting for transfers between devices  192 us
    reduce_scatter x1, waiting for transfers between devices, local(): lax.psum_scatter(partial_out.astype(jnp.bfloat16), 'tensor', scatter_dime...  61.9 us
    all_gather x1, waiting for transfers between devices, local(): gathered = lax.all_gather(frames, 'tensor', axis=1, tiled=True)  50.6 us
    all_gather x1, waiting for transfers between devices, local(): piece = lax.all_gather(mixed_grad, 'tensor', axis=1, tiled=True)  46.2 us
    dot_general x1, matrix products, local(): jnp.einsum('fhqk,fkhd->fqhd', score_grad, key_blocks, preferred_element_t...  32.6 us
    dot_general x7, matrix products, contract(): lax.dot_general(left, right, (((0,), (0,)), ((), ())), preferred_element_...  31.9 us
    dot_general x1, matrix products, local(): jnp.einsum('fhqk,fqhd->fkhd', score_grad, query_blocks, preferred_element...  29.7 us
    psum x1, blocking collectives, local(): lax.psum(term_part.astype(jnp.bfloat16), 'tm').astype(jnp.float32)  29.2 us
  transfers between devices with their start and end apart: 12, of which 8 were waited for; matrix products, arithmetic and copies ran while one was open for 29% of the time, Pallas kernels for 0%

commit v1 on v0

v1 whole, which is shorter than its diff:
```python
import jax
import jax.numpy as jnp
from jax import lax
from jax.experimental import pallas as pl
from jax.experimental.pallas import tpu as pltpu
from jax.sharding import PartitionSpec as P

HD = 128
PATCHES = 512
NT = (((1,), (1,)), ((), ()))
TN = (((0,), (0,)), ((), ()))


def mm(left, right, dims=(((1,), (0,)), ((), ()))):
    return lax.dot_general(left, right, dims, preferred_element_type=jnp.float32)


def from_behind(x, axis, by):
    size = lax.axis_size(axis)
    pairs = [(i, i + by) for i in range(size) if 0 <= i + by < size]
    return lax.ppermute(x, axis, pairs)


def swap(x, axis, bit):
    return lax.ppermute(x, axis, [(i, i ^ bit) for i in range(lax.axis_size(axis))])


def ordered(flag, first, second):
    return jnp.where(
        flag == 0,
        jnp.concatenate([first, second], 1),
        jnp.concatenate([second, first], 1),
    )


def gather_tensor(x, me):
    if lax.axis_size("tensor") != 4:
        return lax.all_gather(x, "tensor", axis=1, tiled=True)
    far = swap(x, "tensor", 2)
    near = swap(x, "tensor", 1)
    far_near = swap(far, "tensor", 1)
    core, chip = me % 2, me // 2
    return ordered(chip, ordered(core, x, near), ordered(core, far, far_near))


def scatter_tensor(x, me):
    if lax.axis_size("tensor") != 4:
        return lax.psum_scatter(x, "tensor", scatter_dimension=1, tiled=True).astype(jnp.float32)
    f32 = jnp.float32
    core, chip = me % 2, me // 2
    quarter = x.shape[1] // 4
    part = [x[:, j * quarter : (j + 1) * quarter] for j in range(4)]
    even = jnp.concatenate([part[0], part[2]], 0)
    odd = jnp.concatenate([part[1], part[3]], 0)
    got = swap(jnp.where(core == 0, odd, even), "tensor", 1)
    own = jnp.where(core == 0, even, odd).astype(f32) + got.astype(f32)
    rows = x.shape[0]
    low, high = own[:rows], own[rows:]
    got = swap(jnp.where(chip == 0, high, low).astype(x.dtype), "tensor", 2)
    return jnp.where(chip == 0, low, high) + got.astype(f32)


def scatter_tm(x, position):
    f32 = jnp.float32
    size = lax.axis_size("tm")
    outer = size // 2
    rows, width = x.shape
    x = x.reshape(outer, 2, rows // size, width)
    side, place = position % 2, position // 2
    keep = lax.dynamic_index_in_dim(x, side, 1, keepdims=False)
    give = lax.dynamic_index_in_dim(x, 1 - side, 1, keepdims=False)
    acc = (keep.astype(f32) + swap(give, "tm", 1).astype(f32)).astype(x.dtype)

    def chunk(index):
        return lax.dynamic_index_in_dim(acc, jnp.clip(index, 0, outer - 1), 0, keepdims=False)

    right = left = None
    for step in range(outer - 1):
        reach = outer - 1 - step
        send_right, send_left = chunk(place + reach), chunk(place - reach)
        if right is not None:
            send_right = (send_right.astype(f32) + right.astype(f32)).astype(x.dtype)
            send_left = (send_left.astype(f32) + left.astype(f32)).astype(x.dtype)
        to_right = [(o, o + 1) for o in range(step + 1)]
        to_left = [(outer - 1 - a, outer - 1 - b) for a, b in to_right]
        both = range(2)
        right = lax.ppermute(
            send_right, "tm", [(2 * a + s, 2 * b + s) for a, b in to_right for s in both]
        )
        left = lax.ppermute(
            send_left, "tm", [(2 * a + s, 2 * b + s) for a, b in to_left for s in both]
        )
    total = chunk(place).astype(f32)
    if right is not None:
        total = total + right.astype(f32) + left.astype(f32)
    return total


def pair_probs(cut_ref, query, key_a, key_b):
    scale = HD ** (-0.5)
    score_a = mm(query, key_a, NT) * scale
    score_b = mm(query, key_b, NT) * scale
    score_b = jnp.where(cut_ref[0] != 0, -1e30, score_b)
    top = jnp.maximum(
        jnp.max(score_a, axis=-1, keepdims=True), jnp.max(score_b, axis=-1, keepdims=True)
    )
    exp_a, exp_b = jnp.exp(score_a - top), jnp.exp(score_b - top)
    total = jnp.sum(exp_a, axis=-1, keepdims=True) + jnp.sum(exp_b, axis=-1, keepdims=True)
    inverse = 1.0 / total
    return exp_a * inverse, exp_b * inverse


def forward_kernel(cut_ref, q_ref, ka_ref, kb_ref, va_ref, vb_ref, out_ref):
    prob_a, prob_b = pair_probs(cut_ref, q_ref[...], ka_ref[...], kb_ref[...])
    out = mm(prob_a.astype(jnp.bfloat16), va_ref[...]) + mm(
        prob_b.astype(jnp.bfloat16), vb_ref[...]
    )
    out_ref[...] = out.astype(jnp.bfloat16)


def backward_kernel(
    cut_ref, q_ref, ka_ref, kb_ref, va_ref, vb_ref, do_ref,
    dq_ref, dka_ref, dkb_ref, dva_ref, dvb_ref,
):
    bf16 = jnp.bfloat16
    query, out_grad = q_ref[...], do_ref[...]
    prob_a, prob_b = pair_probs(cut_ref, query, ka_ref[...], kb_ref[...])
    grad_a, grad_b = mm(out_grad, va_ref[...], NT), mm(out_grad, vb_ref[...], NT)
    dva_ref[...] = mm(prob_a.astype(bf16), out_grad, TN).astype(bf16)
    dvb_ref[...] = mm(prob_b.astype(bf16), out_grad, TN).astype(bf16)
    delta = jnp.sum(grad_a * prob_a, axis=-1, keepdims=True) + jnp.sum(
        grad_b * prob_b, axis=-1, keepdims=True
    )
    scale = HD ** (-0.5)
    score_a = (prob_a * (grad_a - delta) * scale).astype(bf16)
    score_b = (prob_b * (grad_b - delta) * scale).astype(bf16)
    dq_ref[...] = (mm(score_a, ka_ref[...]) + mm(score_b, kb_ref[...])).astype(bf16)
    dka_ref[...] = mm(score_a, query, TN).astype(bf16)
    dkb_ref[...] = mm(score_b, query, TN).astype(bf16)


def attention(kernel, outputs, cut, *arrays):
    rows, width = arrays[0].shape
    block = pl.BlockSpec((rows, HD), lambda head: (0, head))
    shape = jax.ShapeDtypeStruct((rows, width), jnp.bfloat16)
    work = 4 if outputs == 1 else 10
    return pl.pallas_call(
        kernel,
        grid=(width // HD,),
        in_specs=[pl.BlockSpec(memory_space=pltpu.SMEM)] + [block] * len(arrays),
        out_specs=[block] * outputs,
        out_shape=[shape] * outputs,
        compiler_params=pltpu.CompilerParams(vmem_limit_bytes=40 * 1024 * 1024),
        cost_estimate=pl.CostEstimate(
            flops=2 * work * rows * rows * width,
            bytes_accessed=2 * rows * width * (len(arrays) + outputs),
            transcendentals=2 * rows * rows * (width // HD),
        ),
    )(cut, *arrays)


def local(
    frames,
    w_query,
    w_key,
    w_value,
    w_out,
    head_gain,
    reward_weight,
    term_weight,
    out_grad,
    reward_bins,
    episode_flags,
):
    f32 = jnp.float32
    bf16 = jnp.bfloat16
    highest = lax.Precision.HIGHEST
    rows, local_width = frames.shape
    span = PATCHES
    pairs = rows // span
    width = w_query.shape[1]
    full_width = w_out.shape[1]
    tm_count = lax.axis_size("tm")
    position = lax.axis_index("tm")
    is_last = position == tm_count - 1
    frame_total = tm_count * pairs
    me = lax.axis_index("tensor")
    none = jnp.zeros((1,), jnp.int32)
    cuts = [none] * (pairs - 1) + [is_last.astype(jnp.int32).reshape(1)]
    feats = [
        gather_tensor(frames[index * span : (index + 1) * span], me) for index in range(pairs)
    ]
    keys = [mm(feat, w_key).astype(bf16) for feat in feats[:1]]
    values = [mm(feat, w_value).astype(bf16) for feat in feats[:1]]
    ahead = from_behind(jnp.concatenate([keys[0], values[0]], 1), "tm", -1)
    keys += [mm(feat, w_key).astype(bf16) for feat in feats[1:]] + [ahead[:, :width]]
    values += [mm(feat, w_value).astype(bf16) for feat in feats[1:]] + [ahead[:, width:]]
    queries = [mm(feat, w_query).astype(bf16) for feat in feats]
    late_grad, _ = lax.optimization_barrier((out_grad, feats[-1]))
    all_out_grad = lax.all_gather(late_grad, "tensor", axis=1, tiled=True)
    attended, mixed = [], []
    for index in range(pairs):
        (heads_out,) = attention(
            forward_kernel,
            1,
            cuts[index],
            queries[index],
            keys[index],
            keys[index + 1],
            values[index],
            values[index + 1],
        )
        attended.append(heads_out)
        summed = scatter_tensor(mm(heads_out, w_out).astype(bf16), me)
        own = frames[index * span : (index + 1) * span].astype(f32)
        mixed.append((own + summed).astype(bf16))
    mixed = jnp.concatenate(mixed, 0)
    attended = jnp.concatenate(attended, 0)
    gathered = jnp.concatenate(feats, 0)
    pooled = mixed.astype(f32).reshape(pairs, span, local_width).mean(axis=1)
    gained = pooled * head_gain[None, :]
    square_part = jnp.sum(pooled * pooled, axis=-1)
    raw_reward = jnp.dot(gained, reward_weight, precision=highest)
    raw_term = jnp.dot(gained, term_weight, precision=highest)
    sums = lax.psum(
        jnp.concatenate([raw_reward, raw_term[:, None], square_part[:, None]], 1), "tensor"
    )
    bins_count = reward_weight.shape[1]
    scale = lax.rsqrt(sums[:, bins_count + 1] / full_width + 1e-05)
    reward_logits = scale[:, None] * sums[:, :bins_count]
    term_logit = scale * sums[:, bins_count]
    frame_ids = position * pairs + jnp.arange(pairs, dtype=jnp.int32)
    live = ((episode_flags != 2) & (frame_ids < frame_total - 1)).astype(f32)
    target = (episode_flags == 1).astype(f32)
    onehot = (reward_bins[:, None] == jnp.arange(bins_count, dtype=jnp.int32)[None, :]).astype(f32)
    reward_loss = live * (
        jax.scipy.special.logsumexp(reward_logits, axis=-1)
        - jnp.sum(onehot * reward_logits, axis=-1)
    )
    term_loss = live * (jax.nn.softplus(term_logit) - target * term_logit)
    pair_losses = jnp.stack([reward_loss, term_loss])
    logit_grad = live[:, None] * (jax.nn.softmax(reward_logits, axis=-1) - onehot)
    term_grad = live * (jax.nn.sigmoid(term_logit) - target)
    scale_grad = (jnp.sum(logit_grad * reward_logits, axis=-1) + term_grad * term_logit) / scale
    gain_input_grad = scale[:, None] * (
        jnp.dot(logit_grad, reward_weight.T, precision=highest)
        + term_grad[:, None] * term_weight[None, :]
    )
    pooled_grad = (
        head_gain[None, :] * gain_input_grad
        - (scale_grad * scale**3)[:, None] * pooled / full_width
    )
    reward_part = jnp.dot(gained.T, scale[:, None] * logit_grad, precision=highest)
    term_part = jnp.dot(gained.T, scale * term_grad, precision=highest)
    gain_part = jnp.sum(pooled * gain_input_grad, axis=0)
    all_pooled_grad = lax.all_gather(pooled_grad, "tensor", axis=1, tiled=True)
    piece = (
        (
            all_out_grad.astype(f32).reshape(pairs, span, full_width)
            + all_pooled_grad[:, None, :] / span
        )
        .reshape(rows, full_width)
        .astype(bf16)
    )
    attended_grad = mm(piece, w_out, NT).astype(bf16)
    grads = [None] * pairs
    for index in reversed(range(pairs)):
        grads[index] = attention(
            backward_kernel,
            5,
            cuts[index],
            queries[index],
            keys[index],
            keys[index + 1],
            values[index],
            values[index + 1],
            attended_grad[index * span : (index + 1) * span],
        )
        if index == pairs - 1:
            passed = from_behind(jnp.concatenate([grads[index][2], grads[index][4]], 1), "tm", 1)
    grad_out = scatter_tm(mm(piece, attended, TN).astype(bf16), position).T
    small = lax.psum(
        jnp.concatenate([reward_part, term_part[:, None], gain_part[:, None]], 1).astype(bf16),
        "tm",
    ).astype(f32)
    grad_reward, grad_term, grad_gain = (
        small[:, :bins_count],
        small[:, bins_count],
        small[:, bins_count + 1],
    )
    query_grad = jnp.concatenate([grad[0] for grad in grads], 0)
    grad_query = scatter_tm(mm(gathered, query_grad, TN).astype(bf16), position)

    def joined(first, second, behind):
        late = [behind] + [grad[second] for grad in grads[:-1]]
        return jnp.concatenate(
            [
                (grad[first].astype(f32) + other.astype(f32)).astype(bf16)
                for grad, other in zip(grads, late)
            ],
            0,
        )

    value_grad = joined(3, 4, passed[:, width:])
    grad_value = scatter_tm(mm(gathered, value_grad, TN).astype(bf16), position)
    key_grad = joined(1, 2, passed[:, :width])
    grad_key = scatter_tm(mm(gathered, key_grad, TN).astype(bf16), position)
    return (
        mixed,
        pair_losses,
        grad_query,
        grad_key,
        grad_value,
        grad_out,
        grad_reward,
        grad_term,
        grad_gain,
    )


def solution(mesh):
    return jax.shard_map(
        local,
        mesh=mesh,
        in_specs=(
            P("tm", "tensor"),
            P(None, "tensor"),
            P(None, "tensor"),
            P(None, "tensor"),
            P("tensor", None),
            P("tensor"),
            P("tensor", None),
            P("tensor"),
            P("tm", "tensor"),
            P("tm"),
            P("tm"),
        ),
        out_specs=(
            P("tm", "tensor"),
            P(None, "tm"),
            P("tm", "tensor"),
            P("tm", "tensor"),
            P("tm", "tensor"),
            P("tensor", "tm"),
            P("tensor", None),
            P("tensor"),
            P("tensor"),
        ),
        check_vma=False,
    )
```

time: 675 us -> 471 us (0.70)
  waiting for transfers between devices: 357 us -> 188 us
  matrix products: 177 us -> 40 us
  starting transfers between devices: 18.6 us -> 89.8 us
  other arithmetic: 15.3 us -> 50.8 us
  Pallas kernels: 0 us -> 33.7 us
  blocking collectives: 40.6 us -> 11.4 us
  local copies, waits for them, and re-layouts: 44.9 us -> 32.1 us
    unnamed x12 -> x2, waiting for transfers between devices: 192 us -> 0.03 us
    ppermute x0 -> x38, waiting for transfers between devices: none -> 138 us  [the longest x14 106 us: swap(): lax.ppermute(x, axis, [(i, i ^ bit) for i in range(lax.axis_size(axis))])]
    dot_general x18 -> x13, matrix products: 161 us -> 35.3 us  [mm(): lax.dot_general(left, right, dims, preferred_element_type=jnp.float32)]
    all_gather x2 -> x1, waiting for transfers between devices: 96.8 us -> 0.02 us  [local(): all_out_grad = lax.all_gather(late_grad, 'tensor', axis=1, tiled=True)]
    ppermute x0 -> x38, starting transfers between devices: none -> 84.9 us  [the longest x12 58.1 us: scatter_tm(): lax.ppermute(send_right, 'tm', [(2 * a + s, 2 * b + s) for a, b in to_rig...]
    reduce_scatter x1 -> x0, waiting for transfers between devices: 61.9 us -> none  [local(): lax.psum_scatter(partial_out.astype(jnp.bfloat16), 'tensor', scatter_dime...]
    ppermute x4 -> x2, waiting for transfers between devices: 6.89 us -> 49.9 us  [from_behind(): return lax.ppermute(x, axis, pairs)]
    psum x3 -> x1, blocking collectives: 40.6 us -> 6.2 us  [local(): lax.psum(jnp.concatenate([raw_reward, raw_term[:, None], square_part[:, N...]
  transfers between devices with their start and end apart: 12 -> 42, of which waited for: 8 -> 15; matrix products, arithmetic and copies ran while one was open for 29% -> 21% of each run, Pallas kernels for 0% -> 7%
where the time goes in v1:
time: 471 us; the launch traced here: 463 us
  waiting for transfers between devices  188 us (40%)
  starting transfers between devices  89.8 us (19%)
  other arithmetic  50.8 us (11%)
  matrix products  40 us (8%)
  Pallas kernels  33.7 us (7%)
  local copies, waits for them, and re-layouts  32.1 us (7%)
  between operations  17 us (4%)
  blocking collectives  11.4 us (2%)
    ppermute x14, waiting for transfers between devices, swap(): lax.ppermute(x, axis, [(i, i ^ bit) for i in range(lax.axis_size(axis))])  106 us
    ppermute x12, starting transfers between devices, scatter_tm(): lax.ppermute(send_right, 'tm', [(2 * a + s, 2 * b + s) for a, b in to_rig...  58.1 us
    ppermute x2, waiting for transfers between devices, from_behind(): return lax.ppermute(x, axis, pairs)  49.9 us
    dot_general x13, matrix products, mm(): lax.dot_general(left, right, dims, preferred_element_type=jnp.float32)  35.3 us
    pallas_call x4, Pallas kernels, attention(): pl.pallas_call(kernel, grid=(width // HD,), in_specs=[pl.BlockSpec(memory...  33.7 us
    ppermute x12, waiting for transfers between devices, scatter_tm(): lax.ppermute(send_right, 'tm', [(2 * a + s, 2 * b + s) for a, b in to_rig...  19.2 us
    unnamed x109, local copies, waits for them, and re-layouts  15.2 us
    ppermute x14, starting transfers between devices, swap(): lax.ppermute(x, axis, [(i, i ^ bit) for i in range(lax.axis_size(axis))])  15.1 us
  transfers between devices with their start and end apart: 42, of which 15 were waited for; matrix products, arithmetic and copies ran while one was open for 21% of the time, Pallas kernels for 7%

profile of v1, /device:TPU:0, one launch (start us, length us, event | category | flops | bytes accessed | tf_op | source)
XLA Modules:
  0.0 462.8 jit_solution(3208843949636897821)
XLA Ops:
  8.1 2.8 fusion.65
  10.8 3.0 collective-permute-start.1
  14.3 18.1 %collective-permute-done.1 = bf16[512,768]{1,0:T(8,128)(2,1)} collective-permute-done((bf16[512,768]{1,0:T(8,128)(2,1)}, bf16[512,768]{1,0:T(8,128)(2,1)}, u32[]{:S(2)}, u32[]{:S(2)}) %collective-permute-start.1) | collective-permute-done | bytes 786464 | tf_op jit(solution)/shard_map/ppermute | solution.py:25
  32.5 16.0 %collective-permute-done.4 = bf16[512,768]{1,0:T(8,128)(2,1)} collective-permute-done((bf16[512,768]{1,0:T(8,128)(2,1)}, bf16[512,768]{1,0:T(8,128)(2,1)}, u32[]{:S(2)}, u32[]{:S(2)}) %collective-permute-start.4) | collective-permute-done | bytes 786464 | tf_op jit(solution)/shard_map/ppermute | solution.py:25
  48.5 2.3 maximum_select_fusion.2
  61.9 2.6 convolution_convert_fusion.10.kb_ref.ka_ref
  66.9 2.6 convolution_convert_fusion.8.vb_ref.va_ref
  69.6 2.6 convolution_convert_fusion.12.q_ref
  80.0 7.0 %shard_map.178 = bf16[512,512]{1,0:T(8,128)(2,1)S(1)} custom-call(s32[1]{0:T(128)} %constant.182.clone.1.cut_ref, bf16[512,512]{1,0:T(8,128)(2,1)S(1)} %copy-done.20, bf16[512,512]{1,0:T(8,128)(2,1)S(1)} %copy-done.3, bf16[512,512]{1,0:T(8,128)(2,1)S(1)} %copy-done.14, bf16[512,512]{1,0:T(8,128)(2,1)S(1)} %copy-done.6, bf16[512,512]{1,0:T(8,128)(2,1)S(1)} %copy-done.17), custom_call_target="tpu_custom_call" | custom-call | flops 1073741824 | bytes 3145728 | tf_op jit(solution)/shard_map/pallas_call | solution.py:147
  93.7 7.3 %collective-permute-done.8 = bf16[512,1024]{1,0:T(8,128)(2,1)} collective-permute-done((bf16[512,1024]{1,0:T(8,128)(2,1)}, bf16[512,1024]{1,0:T(8,128)(2,1)}, u32[]{:S(2)}, u32[]{:S(2)}) %collective-permute-start.8) | collective-permute-done | bytes 1048608 | tf_op jit(solution)/shard_map/ppermute | solution.py:21
  102.3 7.1 %shard_map.179 = bf16[512,512]{1,0:T(8,128)(2,1)S(1)} custom-call(s32[1]{0:T(128)} %bitcast.cut_ref, bf16[512,512]{1,0:T(8,128)(2,1)S(1)} %convolution_convert_fusion.7.q_ref, bf16[512,512]{1,0:T(8,128)(2,1)S(1)} %copy-done.15, bf16[512,512]{1,0:T(8,128)(2,1)S(1)} %get-tuple-element.98.kb_ref, bf16[512,512]{1,0:T(8,128)(2,1)S(1)} %copy-done.18, ...), custom_call_target="tpu_custom_call" | custom-call | flops 1073741824 | bytes 3145728 | tf_op jit(solution)/shard_map/pallas_call | solution.py:147
  119.6 20.5 %collective-permute-done.7 = bf16[512,768]{1,0:T(8,128)(2,1)} collective-permute-done((bf16[512,768]{1,0:T(8,128)(2,1)}, bf16[512,768]{1,0:T(8,128)(2,1)}, u32[]{:S(2)}, u32[]{:S(2)}) %collective-permute-start.7) | collective-permute-done | bytes 786464 | tf_op jit(solution)/shard_map/ppermute | solution.py:25
  140.1 16.7 %collective-permute-done.10 = bf16[512,768]{1,0:T(8,128)(2,1)} collective-permute-done((bf16[512,768]{1,0:T(8,128)(2,1)}, bf16[512,768]{1,0:T(8,128)(2,1)}, u32[]{:S(2)}, u32[]{:S(2)}) %collective-permute-start.10) | collective-permute-done | bytes 786464 | tf_op jit(solution)/shard_map/ppermute | solution.py:25
  156.8 4.4 add_convert_fusion.1
  164.7 6.2 %psum.14 = f32[2,257]{1,0:T(2,128)S(1)} all-reduce(f32[2,257]{1,0:T(2,128)S(1)} %pad_maximum_fusion.12), channel_id=1, replica_groups=mesh['tm'=8,'tensor'=4] {'tensor'}, use_global_device_ids=true, to_apply=%region_2.3 | all-reduce | flops 514 | bytes 4112 | tf_op jit(solution)/shard_map/psum | solution.py:225
  173.8 5.2 %all_gather.7 = f32[2,3072]{1,0:T(2,128)S(1)} all-gather(f32[2,768]{1,0:T(2,128)S(1)} %get-tuple-element.100), channel_id=1, replica_groups=mesh['tm'=8,'tensor'=4] {'tensor'}, dimensions={1}, use_global_device_ids=true | all-gather | bytes 30720 | tf_op jit(solution)/shard_map/all_gather | solution.py:256
  180.8 4.4 fusion
  185.2 3.4 convolution_convert_fusion.6
  188.8 9.8 %shard_map.181 = (bf16[512,512]{1,0:T(8,128)(2,1)S(1)}, bf16[512,512]{1,0:T(8,128)(2,1)S(1)}, bf16[512,512]{1,0:T(8,128)(2,1)S(1)}, bf16[512,512]{1,0:T(8,128)(2,1)S(1)}, bf16[512,512]{1,0:T(8,128)(2,1)S(1)}) custom-call(s32[1]{0:T(128)} %bitcast.cut_ref, bf16[512,512]{1,0:T(8,128)(2,1)S(1)} %copy-done.25, bf16[512,512]{1,0:T(8,128)(2,1)S(1)} %copy-done.16, ...), custom_call_target="tpu_custom_call" | custom-call | flops 2684354560 | bytes 5767168 | tf_op jit(solution)/shard_map/pallas_call | solution.py:147
  198.7 9.8 %shard_map.180 = (bf16[512,512]{1,0:T(8,128)(2,1)S(1)}, bf16[512,512]{1,0:T(8,128)(2,1)S(1)}, bf16[512,512]{1,0:T(8,128)(2,1)S(1)}, bf16[512,512]{1,0:T(8,128)(2,1)S(1)}, bf16[512,512]{1,0:T(8,128)(2,1)S(1)}) custom-call(s32[1]{0:T(128)} %constant.182.clone.1.cut_ref, bf16[512,512]{1,0:T(8,128)(2,1)S(1)} %copy-done.21, bf16[512,512]{1,0:T(8,128)(2,1)S(1)} %copy-done.4, ...), custom_call_target="tpu_custom_call" | custom-call | flops 2684354560 | bytes 5767168 | tf_op jit(solution)/shard_map/pallas_call | solution.py:147
  208.6 3.7 convolution_convert_fusion.3
  216.4 3.3 collective-permute-start.18
  219.7 3.9 convolution_convert_fusion
  225.5 2.6 copy.38
  229.7 2.6 copy.45
  232.6 42.6 %collective-permute-done.18 = bf16[512,1024]{1,0:T(8,128)(2,1)} collective-permute-done((bf16[512,1024]{1,0:T(8,128)(2,1)}, bf16[512,1024]{1,0:T(8,128)(2,1)}, u32[]{:S(2)}, u32[]{:S(2)}) %collective-permute-start.18) | collective-permute-done | bytes 1048608 | tf_op jit(solution)/shard_map/ppermute | solution.py:21
  276.7 3.8 convolution_convert_fusion.2
  281.9 2.5 collective-permute-start.19
  284.4 3.7 convolution_convert_fusion.1
  288.2 3.0 fusion.4
  291.3 3.4 collective-permute-start.12
  294.7 14.2 %collective-permute-done.33 = bf16[4,384,512]{1,2,0:T(8,128)(2,1)} collective-permute-done((bf16[4,384,512]{1,2,0:T(8,128)(2,1)}, bf16[4,384,512]{1,2,0:T(8,128)(2,1)}, u32[]{:S(2)}, u32[]{:S(2)}) %collective-permute-start.33) | collective-permute-done | bytes 1572896 | tf_op jit(solution)/shard_map/ppermute | solution.py:25
  311.7 4.0 collective-permute-start.34
  323.1 5.1 %collective-permute-start.13 = (bf16[384,512]{1,0:T(8,128)(2,1)}, bf16[384,512]{1,0:T(8,128)(2,1)}, u32[]{:S(2)}, u32[]{:S(2)}) collective-permute-start(bf16[384,512]{1,0:T(8,128)(2,1)} %fusion.36), channel_id=1, source_target_pairs={{0,8},{4,12},{8,16},{12,20},{1,9},{5,13},{9,17},{13,21},{2,10},{6,... | collective-permute-start | bytes 1179656 | tf_op jit(solution)/shard_map/ppermute | solution.py:87
  334.4 2.3 copy.39
  339.7 6.4 %collective-permute-start.14 = (bf16[384,512]{1,0:T(8,128)(2,1)S(1)}, bf16[384,512]{1,0:T(8,128)(2,1)S(1)}, u32[]{:S(2)}, u32[]{:S(2)}) collective-permute-start(bf16[384,512]{1,0:T(8,128)(2,1)S(1)} %get-tuple-element.85), channel_id=1, source_target_pairs={{0,8},{4,12},{8,16},{12,20},{16,24},{20,28},{1,9},{5,13},{9,17},{1... | collective-permute-start | bytes 1179656 | tf_op jit(solution)/shard_map/ppermute | solution.py:87
  350.2 5.2 %collective-permute-start.20 = (bf16[384,512]{1,0:T(8,128)(2,1)S(1)}, bf16[384,512]{1,0:T(8,128)(2,1)S(1)}, u32[]{:S(2)}, u32[]{:S(2)}) collective-permute-start(bf16[384,512]{1,0:T(8,128)(2,1)S(1)} %get-tuple-element.83), channel_id=1, source_target_pairs={{0,8},{4,12},{1,9},{5,13},{2,10},{6,14},{3,11},{7,15}} | collective-permute-start | bytes 1179656 | tf_op jit(solution)/shard_map/ppermute | solution.py:87
  355.5 20.3 %collective-permute-done.26 = bf16[4,384,512]{2,1,0:T(8,128)(2,1)} collective-permute-done((bf16[4,384,512]{2,1,0:T(8,128)(2,1)}, bf16[4,384,512]{2,1,0:T(8,128)(2,1)}, u32[]{:S(2)}, u32[]{:S(2)}) %collective-permute-start.26) | collective-permute-done | bytes 1572896 | tf_op jit(solution)/shard_map/ppermute | solution.py:25
  378.3 4.0 collective-permute-start.27
  383.3 7.1 %collective-permute-done.27 = bf16[384,512]{1,0:T(8,128)(2,1)S(1)} collective-permute-done((bf16[384,512]{1,0:T(8,128)(2,1)S(1)}, bf16[384,512]{1,0:T(8,128)(2,1)S(1)}, u32[]{:S(2)}, u32[]{:S(2)}) %collective-permute-start.27) | collective-permute-done | bytes 393248 | tf_op jit(solution)/shard_map/ppermute | solution.py:87
  390.4 4.4 collective-permute-start.21
  399.1 5.2 %collective-permute-done.21 = bf16[384,512]{1,0:T(8,128)(2,1)S(1)} collective-permute-done((bf16[384,512]{1,0:T(8,128)(2,1)S(1)}, bf16[384,512]{1,0:T(8,128)(2,1)S(1)}, u32[]{:S(2)}, u32[]{:S(2)}) %collective-permute-start.21) | collective-permute-done | bytes 393248 | tf_op jit(solution)/shard_map/ppermute | solution.py:87
  407.1 5.6 %collective-permute-done.28 = bf16[384,512]{1,0:T(8,128)(2,1)S(1)} collective-permute-done((bf16[384,512]{1,0:T(8,128)(2,1)S(1)}, bf16[384,512]{1,0:T(8,128)(2,1)S(1)}, u32[]{:S(2)}, u32[]{:S(2)}) %collective-permute-start.28) | collective-permute-done | bytes 393248 | tf_op jit(solution)/shard_map/ppermute | solution.py:87
  414.3 3.1 collective-permute-done.17
  418.4 5.2 %collective-permute-start.22 = (bf16[384,512]{1,0:T(8,128)(2,1)S(1)}, bf16[384,512]{1,0:T(8,128)(2,1)S(1)}, u32[]{:S(2)}, u32[]{:S(2)}) collective-permute-start(bf16[384,512]{1,0:T(8,128)(2,1)S(1)} %get-tuple-element.81), channel_id=1, source_target_pairs={{0,8},{4,12},{8,16},{12,20},{16,24},{20,28},{1,9},{5,13},{9,17},{1... | collective-permute-start | bytes 1179656 | tf_op jit(solution)/shard_map/ppermute | solution.py:87
  423.7 14.2 %collective-permute-start.29 = (bf16[384,512]{1,0:T(8,128)(2,1)S(1)}, bf16[384,512]{1,0:T(8,128)(2,1)S(1)}, u32[]{:S(2)}, u32[]{:S(2)}) collective-permute-start(bf16[384,512]{1,0:T(8,128)(2,1)S(1)} %get-tuple-element.77), channel_id=1, source_target_pairs={{0,8},{4,12},{8,16},{12,20},{16,24},{20,28},{1,9},{5,13},{9,17},{1... | collective-permute-start | bytes 1179656 | tf_op jit(solution)/shard_map/ppermute | solution.py:87
  443.1 6.8 %collective-permute-done.25 = bf16[384,512]{1,0:T(8,128)(2,1)S(1)} collective-permute-done((bf16[384,512]{1,0:T(8,128)(2,1)S(1)}, bf16[384,512]{1,0:T(8,128)(2,1)S(1)}, u32[]{:S(2)}, u32[]{:S(2)}) %collective-permute-start.25) | collective-permute-done | bytes 393248 | tf_op jit(solution)/shard_map/ppermute | solution.py:90
  450.9 3.2 collective-permute-done.32
  (244 shorter events, 102.6 us)
Async XLA Ops:
  8.0 79.1 %copy-start = (bf16[512,3072]{1,0:T(8,128)(2,1)S(1)}, bf16[512,3072]{1,0:T(8,128)(2,1)}, u32[]{:S(2)}) copy-start(bf16[512,3072]{1,0:T(8,128)(2,1)} %param.15) | copy-start | bytes 9437188
  8.0 172.8 %all-gather.2.cloned.1.call-start = ((), (), s32[]{:S(2)}) async-start(), calls=%async_computation | async-start | bytes 7864320 | tf_op jit(solution)/shard_map/all_gather | solution.py:200
  10.8 21.6 %collective-permute-start.1 = (bf16[512,768]{1,0:T(8,128)(2,1)}, bf16[512,768]{1,0:T(8,128)(2,1)}, u32[]{:S(2)}, u32[]{:S(2)}) collective-permute-start(bf16[512,768]{1,0:T(8,128)(2,1)} %get-tuple-element.91), channel_id=1, source_target_pairs={{0,2},{1,3},{2,0},{3,1},{4,6},{5,7},{6,4},{7,5},{8,10},{9,11},{10,... | collective-permute-start | bytes 2359304 | tf_op jit(solution)/shard_map/ppermute | solution.py:25
  13.8 34.7 %collective-permute-start.4 = (bf16[512,768]{1,0:T(8,128)(2,1)}, bf16[512,768]{1,0:T(8,128)(2,1)}, u32[]{:S(2)}, u32[]{:S(2)}) collective-permute-start(bf16[512,768]{1,0:T(8,128)(2,1)} %get-tuple-element.92), channel_id=1, source_target_pairs={{0,2},{1,3},{2,0},{3,1},{4,6},{5,7},{6,4},{7,5},{8,10},{9,11},{10,... | collective-permute-start | bytes 2359304 | tf_op jit(solution)/shard_map/ppermute | solution.py:25
  13.8 34.7 %collective-permute-start = (bf16[512,768]{1,0:T(8,128)(2,1)}, bf16[512,768]{1,0:T(8,128)(2,1)}, u32[]{:S(2)}, u32[]{:S(2)}) collective-permute-start(bf16[512,768]{1,0:T(8,128)(2,1)} %get-tuple-element.91), channel_id=1, source_target_pairs={{0,1},{1,0},{2,3},{3,2},{4,5},{5,4},{6,7},{7,6},{8,9},{9,8},{10,11... | collective-permute-start | bytes 2359304 | tf_op jit(solution)/shard_map/ppermute | solution.py:25
  13.8 37.0 %collective-permute-start.3 = (bf16[512,768]{1,0:T(8,128)(2,1)}, bf16[512,768]{1,0:T(8,128)(2,1)}, u32[]{:S(2)}, u32[]{:S(2)}) collective-permute-start(bf16[512,768]{1,0:T(8,128)(2,1)} %get-tuple-element.92), channel_id=1, source_target_pairs={{0,1},{1,0},{2,3},{3,2},{4,5},{5,4},{6,7},{7,6},{8,9},{9,8},{10,11... | collective-permute-start | bytes 2359304 | tf_op jit(solution)/shard_map/ppermute | solution.py:25
  32.5 20.6 %collective-permute-start.2 = (bf16[512,768]{1,0:T(8,128)(2,1)}, bf16[512,768]{1,0:T(8,128)(2,1)}, u32[]{:S(2)}, u32[]{:S(2)}) collective-permute-start(bf16[512,768]{1,0:T(8,128)(2,1)} %collective-permute-done.1), channel_id=1, source_target_pairs={{0,1},{1,0},{2,3},{3,2},{4,5},{5,4},{6,7},{7,6},{8,9},{9,8},{10,11... | collective-permute-start | bytes 2359304 | tf_op jit(solution)/shard_map/ppermute | solution.py:25
  48.5 10.5 %collective-permute-start.5 = (bf16[512,768]{1,0:T(8,128)(2,1)}, bf16[512,768]{1,0:T(8,128)(2,1)S(1)}, u32[]{:S(2)}, u32[]{:S(2)}) collective-permute-start(bf16[512,768]{1,0:T(8,128)(2,1)} %collective-permute-done.4), channel_id=1, source_target_pairs={{0,1},{1,0},{2,3},{3,2},{4,5},{5,4},{6,7},{7,6},{8,9},{9,8},{10,11... | collective-permute-start | bytes 2359304 | tf_op jit(solution)/shard_map/ppermute | solution.py:25
  73.2 27.8 %collective-permute-start.8 = (bf16[512,1024]{1,0:T(8,128)(2,1)}, bf16[512,1024]{1,0:T(8,128)(2,1)}, u32[]{:S(2)}, u32[]{:S(2)}) collective-permute-start(bf16[512,1024]{1,0:T(8,128)(2,1)} %pad_maximum_fusion.9), channel_id=1, source_target_pairs={{4,0},{8,4},{12,8},{16,12},{20,16},{24,20},{28,24},{5,1},{9,5},{13... | collective-permute-start | bytes 3145736 | tf_op jit(solution)/shard_map/ppermute | solution.py:21
  74.6 257.9 %all-reduce.2.cloned.1.call-start = ((), (), s32[]{:S(2)}) async-start(), calls=%async_computation.1 | async-start | bytes 811008 | tf_op jit(solution)/shard_map/psum | solution.py:282
  89.5 22.4 %collective-permute-start.6 = (bf16[1024,768]{1,0:T(8,128)(2,1)S(1)}, bf16[1024,768]{1,0:T(8,128)(2,1)S(1)}, u32[]{:S(2)}, u32[]{:S(2)}) collective-permute-start(bf16[1024,768]{1,0:T(8,128)(2,1)S(1)} %broadcast_select_fusion.1), channel_id=1, source_target_pairs={{0,1},{1,0},{2,3},{3,2},{4,5},{5,4},{6,7},{7,6},{8,9},{9,8},{10,11... | collective-permute-start | bytes 4718600 | tf_op jit(solution)/shard_map/ppermute | solution.py:25
  111.8 3.7 collective-permute-start.9
  113.7 26.4 %collective-permute-start.7 = (bf16[512,768]{1,0:T(8,128)(2,1)}, bf16[512,768]{1,0:T(8,128)(2,1)}, u32[]{:S(2)}, u32[]{:S(2)}) collective-permute-start(bf16[512,768]{1,0:T(8,128)(2,1)} %select_convert_fusion.1), channel_id=1, source_target_pairs={{0,2},{1,3},{2,0},{3,1},{4,6},{5,7},{6,4},{7,5},{8,10},{9,11},{10,... | collective-permute-start | bytes 2359304 | tf_op jit(solution)/shard_map/ppermute | solution.py:25
  117.9 38.9 %collective-permute-start.10 = (bf16[512,768]{1,0:T(8,128)(2,1)}, bf16[512,768]{1,0:T(8,128)(2,1)}, u32[]{:S(2)}, u32[]{:S(2)}) collective-permute-start(bf16[512,768]{1,0:T(8,128)(2,1)} %select_convert_fusion), channel_id=1, source_target_pairs={{0,2},{1,3},{2,0},{3,1},{4,6},{5,7},{6,4},{7,5},{8,10},{9,11},{10,... | collective-permute-start | bytes 2359304 | tf_op jit(solution)/shard_map/ppermute | solution.py:25
  213.6 74.6 %collective-permute-start.11 = (bf16[4,384,512]{2,1,0:T(8,128)(2,1)}, bf16[4,384,512]{2,1,0:T(8,128)(2,1)}, u32[]{:S(2)}, u32[]{:S(2)}) collective-permute-start(bf16[4,384,512]{2,1,0:T(8,128)(2,1)} %dynamic-slice_bitcast_fusion.2), channel_id=1, source_target_pairs={{0,4},{4,0},{8,12},{12,8},{16,20},{20,16},{24,28},{28,24},{1,5},{5... | collective-permute-start | bytes 4718600 | tf_op jit(solution)/shard_map/ppermute | solution.py:25
  216.4 58.8 %collective-permute-start.18 = (bf16[512,1024]{1,0:T(8,128)(2,1)}, bf16[512,1024]{1,0:T(8,128)(2,1)}, u32[]{:S(2)}, u32[]{:S(2)}) collective-permute-start(bf16[512,1024]{1,0:T(8,128)(2,1)} %pad_maximum_fusion.10), channel_id=1, source_target_pairs={{0,4},{4,8},{8,12},{12,16},{16,20},{20,24},{24,28},{1,5},{5,9},{9,... | collective-permute-start | bytes 3145736 | tf_op jit(solution)/shard_map/ppermute | solution.py:21
  228.1 80.8 %collective-permute-start.33 = (bf16[4,384,512]{1,2,0:T(8,128)(2,1)}, bf16[4,384,512]{1,2,0:T(8,128)(2,1)}, u32[]{:S(2)}, u32[]{:S(2)}) collective-permute-start(bf16[4,384,512]{1,2,0:T(8,128)(2,1)} %bitcast.159), channel_id=1, source_target_pairs={{0,4},{4,0},{8,12},{12,8},{16,20},{20,16},{24,28},{28,24},{1,5},{5... | collective-permute-start | bytes 4718600 | tf_op jit(solution)/shard_map/ppermute | solution.py:25
  232.3 44.4 %copy-start.33 = (bf16[512,3072]{1,0:T(8,128)(2,1)S(1)}, bf16[512,3072]{1,0:T(8,128)(2,1)}, u32[]{:S(2)}) copy-start(bf16[512,3072]{1,0:T(8,128)(2,1)} %copy-done.31) | copy-start | bytes 9437188
  232.3 44.4 %copy-start.37 = (bf16[512,3072]{1,0:T(8,128)(2,1)S(1)}, bf16[512,3072]{1,0:T(8,128)(2,1)}, u32[]{:S(2)}) copy-start(bf16[512,3072]{1,0:T(8,128)(2,1)} %copy-done.34) | copy-start | bytes 9437188
  281.9 66.3 %collective-permute-start.19 = (bf16[4,384,512]{2,1,0:T(8,128)(2,1)}, bf16[4,384,512]{2,1,0:T(8,128)(2,1)}, u32[]{:S(2)}, u32[]{:S(2)}) collective-permute-start(bf16[4,384,512]{2,1,0:T(8,128)(2,1)} %dynamic-slice_bitcast_fusion.1), channel_id=1, source_target_pairs={{0,4},{4,0},{8,12},{12,8},{16,20},{20,16},{24,28},{28,24},{1,5},{5... | collective-permute-start | bytes 4718600 | tf_op jit(solution)/shard_map/ppermute | solution.py:25
  288.2 27.5 %copy-start.38 = (bf16[3072,512]{1,0:T(8,128)(2,1)}, bf16[3072,512]{1,0:T(8,128)(2,1)S(1)}, u32[]{:S(2)}) copy-start(bf16[3072,512]{1,0:T(8,128)(2,1)S(1)} %convolution_convert_fusion.1) | copy-start | bytes 9437188
  291.3 28.2 %collective-permute-start.12 = (bf16[384,512]{1,0:T(8,128)(2,1)S(1)}, bf16[384,512]{1,0:T(8,128)(2,1)S(1)}, u32[]{:S(2)}, u32[]{:S(2)}) collective-permute-start(bf16[384,512]{1,0:T(8,128)(2,1)S(1)} %get-tuple-element.87), channel_id=1, source_target_pairs={{0,8},{4,12},{1,9},{5,13},{2,10},{6,14},{3,11},{7,15}} | collective-permute-start | bytes 1179656 | tf_op jit(solution)/shard_map/ppermute | solution.py:87
  310.7 86.3 %copy-start.28 = (bf16[4,384,512]{1,2,0:T(8,128)(2,1)}, bf16[4,384,512]{1,2,0:T(8,128)(2,1)S(1)}, u32[]{:S(2)}) copy-start(bf16[4,384,512]{1,2,0:T(8,128)(2,1)S(1)} %fusion.1) | copy-start | bytes 4718596
  311.7 11.4 %collective-permute-start.34 = (bf16[384,512]{0,1:T(8,128)(2,1)S(1)}, bf16[384,512]{0,1:T(8,128)(2,1)S(1)}, u32[]{:S(2)}, u32[]{:S(2)}) collective-permute-start(bf16[384,512]{0,1:T(8,128)(2,1)S(1)} %get-tuple-element.75), channel_id=1, source_target_pairs={{0,8},{4,12},{1,9},{5,13},{2,10},{6,14},{3,11},{7,15}} | collective-permute-start | bytes 1179656 | tf_op jit(solution)/shard_map/ppermute | solution.py:87
  316.9 58.8 %collective-permute-start.26 = (bf16[4,384,512]{2,1,0:T(8,128)(2,1)}, bf16[4,384,512]{2,1,0:T(8,128)(2,1)}, u32[]{:S(2)}, u32[]{:S(2)}) collective-permute-start(bf16[4,384,512]{2,1,0:T(8,128)(2,1)} %dynamic-slice_bitcast_fusion), channel_id=1, source_target_pairs={{0,4},{4,0},{8,12},{12,8},{16,20},{20,16},{24,28},{28,24},{1,5},{5... | collective-permute-start | bytes 4718600 | tf_op jit(solution)/shard_map/ppermute | solution.py:25
  318.8 10.2 %collective-permute-start.15 = (bf16[384,512]{1,0:T(8,128)(2,1)S(1)}, bf16[384,512]{1,0:T(8,128)(2,1)S(1)}, u32[]{:S(2)}, u32[]{:S(2)}) collective-permute-start(bf16[384,512]{1,0:T(8,128)(2,1)S(1)} %get-tuple-element.88), channel_id=1, source_target_pairs={{24,16},{28,20},{25,17},{29,21},{26,18},{30,22},{27,19},{31,23}} | collective-permute-start | bytes 1179656 | tf_op jit(solution)/shard_map/ppermute | solution.py:90
  319.5 20.1 %collective-permute-start.37 = (bf16[384,512]{0,1:T(8,128)(2,1)}, bf16[384,512]{0,1:T(8,128)(2,1)}, u32[]{:S(2)}, u32[]{:S(2)}) collective-permute-start(bf16[384,512]{0,1:T(8,128)(2,1)} %get-tuple-element.76), channel_id=1, source_target_pairs={{24,16},{28,20},{25,17},{29,21},{26,18},{30,22},{27,19},{31,23}} | collective-permute-start | bytes 1179656 | tf_op jit(solution)/shard_map/ppermute | solution.py:90
  323.1 14.3 %collective-permute-start.13 = (bf16[384,512]{1,0:T(8,128)(2,1)}, bf16[384,512]{1,0:T(8,128)(2,1)}, u32[]{:S(2)}, u32[]{:S(2)}) collective-permute-start(bf16[384,512]{1,0:T(8,128)(2,1)} %fusion.36), channel_id=1, source_target_pairs={{0,8},{4,12},{8,16},{12,20},{1,9},{5,13},{9,17},{13,21},{2,10},{6,... | collective-permute-start | bytes 1179656 | tf_op jit(solution)/shard_map/ppermute | solution.py:87
  329.8 16.2 %collective-permute-start.35 = (bf16[384,512]{0,1:T(8,128)(2,1)}, bf16[384,512]{0,1:T(8,128)(2,1)}, u32[]{:S(2)}, u32[]{:S(2)}) collective-permute-start(bf16[384,512]{0,1:T(8,128)(2,1)} %fusion.20), channel_id=1, source_target_pairs={{0,8},{4,12},{8,16},{12,20},{1,9},{5,13},{9,17},{13,21},{2,10},{6,... | collective-permute-start | bytes 1179656 | tf_op jit(solution)/shard_map/ppermute | solution.py:87
  339.0 39.4 %collective-permute-start.16 = (bf16[384,512]{1,0:T(8,128)(2,1)S(1)}, bf16[384,512]{1,0:T(8,128)(2,1)S(1)}, u32[]{:S(2)}, u32[]{:S(2)}) collective-permute-start(bf16[384,512]{1,0:T(8,128)(2,1)S(1)} %get-tuple-element.86), channel_id=1, source_target_pairs={{24,16},{28,20},{16,8},{20,12},{25,17},{29,21},{17,9},{21,13},{26,... | collective-permute-start | bytes 1179656 | tf_op jit(solution)/shard_map/ppermute | solution.py:90
  339.7 73.9 %collective-permute-start.14 = (bf16[384,512]{1,0:T(8,128)(2,1)S(1)}, bf16[384,512]{1,0:T(8,128)(2,1)S(1)}, u32[]{:S(2)}, u32[]{:S(2)}) collective-permute-start(bf16[384,512]{1,0:T(8,128)(2,1)S(1)} %get-tuple-element.85), channel_id=1, source_target_pairs={{0,8},{4,12},{8,16},{12,20},{16,24},{20,28},{1,9},{5,13},{9,17},{1... | collective-permute-start | bytes 1179656 | tf_op jit(solution)/shard_map/ppermute | solution.py:87
  347.4 29.0 %copy-start.39 = (bf16[3072,512]{1,0:T(8,128)(2,1)S(1)}, bf16[3072,512]{1,0:T(8,128)(2,1)}, u32[]{:S(2)}) copy-start(bf16[3072,512]{1,0:T(8,128)(2,1)} %copy-done.38) | copy-start | bytes 9437188
  347.4 47.5 %collective-permute-start.38 = (bf16[384,512]{0,1:T(8,128)(2,1)S(1)}, bf16[384,512]{0,1:T(8,128)(2,1)S(1)}, u32[]{:S(2)}, u32[]{:S(2)}) collective-permute-start(bf16[384,512]{0,1:T(8,128)(2,1)S(1)} %get-tuple-element.74), channel_id=1, source_target_pairs={{24,16},{28,20},{16,8},{20,12},{25,17},{29,21},{17,9},{21,13},{26,... | collective-permute-start | bytes 1179656 | tf_op jit(solution)/shard_map/ppermute | solution.py:90
  350.2 32.2 %collective-permute-start.20 = (bf16[384,512]{1,0:T(8,128)(2,1)S(1)}, bf16[384,512]{1,0:T(8,128)(2,1)S(1)}, u32[]{:S(2)}, u32[]{:S(2)}) collective-permute-start(bf16[384,512]{1,0:T(8,128)(2,1)S(1)} %get-tuple-element.83), channel_id=1, source_target_pairs={{0,8},{4,12},{1,9},{5,13},{2,10},{6,14},{3,11},{7,15}} | collective-permute-start | bytes 1179656 | tf_op jit(solution)/shard_map/ppermute | solution.py:87
  375.7 21.5 %collective-permute-start.23 = (bf16[384,512]{1,0:T(8,128)(2,1)S(1)}, bf16[384,512]{1,0:T(8,128)(2,1)S(1)}, u32[]{:S(2)}, u32[]{:S(2)}) collective-permute-start(bf16[384,512]{1,0:T(8,128)(2,1)S(1)} %get-tuple-element.84), channel_id=1, source_target_pairs={{24,16},{28,20},{25,17},{29,21},{26,18},{30,22},{27,19},{31,23}} | collective-permute-start | bytes 1179656 | tf_op jit(solution)/shard_map/ppermute | solution.py:90
  378.3 12.0 %collective-permute-start.27 = (bf16[384,512]{1,0:T(8,128)(2,1)S(1)}, bf16[384,512]{1,0:T(8,128)(2,1)S(1)}, u32[]{:S(2)}, u32[]{:S(2)}) collective-permute-start(bf16[384,512]{1,0:T(8,128)(2,1)S(1)} %get-tuple-element.79), channel_id=1, source_target_pairs={{0,8},{4,12},{1,9},{5,13},{2,10},{6,14},{3,11},{7,15}} | collective-permute-start | bytes 1179656 | tf_op jit(solution)/shard_map/ppermute | solution.py:87
  382.5 23.3 %collective-permute-start.30 = (bf16[384,512]{1,0:T(8,128)(2,1)S(1)}, bf16[384,512]{1,0:T(8,128)(2,1)S(1)}, u32[]{:S(2)}, u32[]{:S(2)}) collective-permute-start(bf16[384,512]{1,0:T(8,128)(2,1)S(1)} %get-tuple-element.80), channel_id=1, source_target_pairs={{24,16},{28,20},{25,17},{29,21},{26,18},{30,22},{27,19},{31,23}} | collective-permute-start | bytes 1179656 | tf_op jit(solution)/shard_map/ppermute | solution.py:90
  390.4 13.9 %collective-permute-start.21 = (bf16[384,512]{1,0:T(8,128)(2,1)S(1)}, bf16[384,512]{1,0:T(8,128)(2,1)S(1)}, u32[]{:S(2)}, u32[]{:S(2)}) collective-permute-start(bf16[384,512]{1,0:T(8,128)(2,1)S(1)} %fusion.31), channel_id=1, source_target_pairs={{0,8},{4,12},{8,16},{12,20},{1,9},{5,13},{9,17},{13,21},{2,10},{6,... | collective-permute-start | bytes 1179656 | tf_op jit(solution)/shard_map/ppermute | solution.py:87
  394.9 17.8 %collective-permute-start.28 = (bf16[384,512]{1,0:T(8,128)(2,1)S(1)}, bf16[384,512]{1,0:T(8,128)(2,1)S(1)}, u32[]{:S(2)}, u32[]{:S(2)}) collective-permute-start(bf16[384,512]{1,0:T(8,128)(2,1)S(1)} %fusion.26), channel_id=1, source_target_pairs={{0,8},{4,12},{8,16},{12,20},{1,9},{5,13},{9,17},{13,21},{2,10},{6,... | collective-permute-start | bytes 1179656 | tf_op jit(solution)/shard_map/ppermute | solution.py:87
  397.2 42.3 %collective-permute-start.36 = (bf16[384,512]{0,1:T(8,128)(2,1)S(1)}, bf16[384,512]{0,1:T(8,128)(2,1)S(1)}, u32[]{:S(2)}, u32[]{:S(2)}) collective-permute-start(bf16[384,512]{0,1:T(8,128)(2,1)S(1)} %get-tuple-element.73), channel_id=1, source_target_pairs={{0,8},{4,12},{8,16},{12,20},{16,24},{20,28},{1,9},{5,13},{9,17},{1... | collective-permute-start | bytes 1179656 | tf_op jit(solution)/shard_map/ppermute | solution.py:87
  404.3 13.1 %collective-permute-start.17 = (bf16[384,512]{1,0:T(8,128)(2,1)S(1)}, bf16[384,512]{1,0:T(8,128)(2,1)S(1)}, u32[]{:S(2)}, u32[]{:S(2)}) collective-permute-start(bf16[384,512]{1,0:T(8,128)(2,1)S(1)} %fusion.35), channel_id=1, source_target_pairs={{24,16},{28,20},{16,8},{20,12},{8,0},{12,4},{25,17},{29,21},{17,9}... | collective-permute-start | bytes 1179656 | tf_op jit(solution)/shard_map/ppermute | solution.py:90
  405.8 35.2 %collective-permute-start.39 = (bf16[384,512]{0,1:T(8,128)(2,1)S(1)}, bf16[384,512]{0,1:T(8,128)(2,1)S(1)}, u32[]{:S(2)}, u32[]{:S(2)}) collective-permute-start(bf16[384,512]{0,1:T(8,128)(2,1)S(1)} %fusion.19), channel_id=1, source_target_pairs={{24,16},{28,20},{16,8},{20,12},{8,0},{12,4},{25,17},{29,21},{17,9}... | collective-permute-start | bytes 1179656 | tf_op jit(solution)/shard_map/ppermute | solution.py:90
  412.7 10.9 %collective-permute-start.24 = (bf16[384,512]{1,0:T(8,128)(2,1)S(1)}, bf16[384,512]{1,0:T(8,128)(2,1)S(1)}, u32[]{:S(2)}, u32[]{:S(2)}) collective-permute-start(bf16[384,512]{1,0:T(8,128)(2,1)S(1)} %get-tuple-element.82), channel_id=1, source_target_pairs={{24,16},{28,20},{16,8},{20,12},{25,17},{29,21},{17,9},{21,13},{26,... | collective-permute-start | bytes 1179656 | tf_op jit(solution)/shard_map/ppermute | solution.py:90
  413.6 24.4 %collective-permute-start.31 = (bf16[384,512]{1,0:T(8,128)(2,1)S(1)}, bf16[384,512]{1,0:T(8,128)(2,1)S(1)}, u32[]{:S(2)}, u32[]{:S(2)}) collective-permute-start(bf16[384,512]{1,0:T(8,128)(2,1)S(1)} %get-tuple-element.78), channel_id=1, source_target_pairs={{24,16},{28,20},{16,8},{20,12},{25,17},{29,21},{17,9},{21,13},{26,... | collective-permute-start | bytes 1179656 | tf_op jit(solution)/shard_map/ppermute | solution.py:90
  418.4 24.7 %collective-permute-start.22 = (bf16[384,512]{1,0:T(8,128)(2,1)S(1)}, bf16[384,512]{1,0:T(8,128)(2,1)S(1)}, u32[]{:S(2)}, u32[]{:S(2)}) collective-permute-start(bf16[384,512]{1,0:T(8,128)(2,1)S(1)} %get-tuple-element.81), channel_id=1, source_target_pairs={{0,8},{4,12},{8,16},{12,20},{16,24},{20,28},{1,9},{5,13},{9,17},{1... | collective-permute-start | bytes 1179656 | tf_op jit(solution)/shard_map/ppermute | solution.py:87
  423.7 27.2 %collective-permute-start.29 = (bf16[384,512]{1,0:T(8,128)(2,1)S(1)}, bf16[384,512]{1,0:T(8,128)(2,1)S(1)}, u32[]{:S(2)}, u32[]{:S(2)}) collective-permute-start(bf16[384,512]{1,0:T(8,128)(2,1)S(1)} %get-tuple-element.77), channel_id=1, source_target_pairs={{0,8},{4,12},{8,16},{12,20},{16,24},{20,28},{1,9},{5,13},{9,17},{1... | collective-permute-start | bytes 1179656 | tf_op jit(solution)/shard_map/ppermute | solution.py:87
  438.0 11.8 %collective-permute-start.25 = (bf16[384,512]{1,0:T(8,128)(2,1)S(1)}, bf16[384,512]{1,0:T(8,128)(2,1)S(1)}, u32[]{:S(2)}, u32[]{:S(2)}) collective-permute-start(bf16[384,512]{1,0:T(8,128)(2,1)S(1)} %fusion.30), channel_id=1, source_target_pairs={{24,16},{28,20},{16,8},{20,12},{8,0},{12,4},{25,17},{29,21},{17,9}... | collective-permute-start | bytes 1179656 | tf_op jit(solution)/shard_map/ppermute | solution.py:90
  439.5 14.6 %collective-permute-start.32 = (bf16[384,512]{1,0:T(8,128)(2,1)S(1)}, bf16[384,512]{1,0:T(8,128)(2,1)S(1)}, u32[]{:S(2)}, u32[]{:S(2)}) collective-permute-start(bf16[384,512]{1,0:T(8,128)(2,1)S(1)} %fusion.25), channel_id=1, source_target_pairs={{24,16},{28,20},{16,8},{20,12},{8,0},{12,4},{25,17},{29,21},{17,9}... | collective-permute-start | bytes 1179656 | tf_op jit(solution)/shard_map/ppermute | solution.py:90
  (47 other events, 308.9 us)
Sparse Core Ops, SparseCore 0:
  74.7 56.0 all-gather.1
Sparse Core Ops, SparseCore 1:
  180.8 92.1 all-reduce.1

commit v2 on v1

--- a/solution.py
+++ b/solution.py
@@ -25,6 +25,26 @@
     return lax.ppermute(x, axis, [(i, i ^ bit) for i in range(lax.axis_size(axis))])
 
 
+def tie(value, *others):
+    return lax.optimization_barrier((value, *others))[0]
+
+
+def twisted():
+    return lax.axis_size("tensor") == 4 and lax.axis_size("tm") == 8
+
+
+def twist_rows(weight, me):
+    if not twisted():
+        return weight
+    quarter = weight.shape[0] // 4
+    return jnp.concatenate(
+        [
+            lax.dynamic_slice_in_dim(weight, (me ^ j) * quarter, quarter, 0) for j in range(4)
+        ],
+        0,
+    )
+
+
 def ordered(flag, first, second):
     return jnp.where(
         flag == 0,
@@ -35,17 +55,22 @@
 
 def gather_tensor(x, me):
     if lax.axis_size("tensor") != 4:
-        return lax.all_gather(x, "tensor", axis=1, tiled=True)
+        return lambda *_: lax.all_gather(x, "tensor", axis=1, tiled=True), x
     far = swap(x, "tensor", 2)
     near = swap(x, "tensor", 1)
-    far_near = swap(far, "tensor", 1)
-    core, chip = me % 2, me // 2
-    return ordered(chip, ordered(core, x, near), ordered(core, far, far_near))
-
-
-def scatter_tensor(x, me):
-    if lax.axis_size("tensor") != 4:
-        return lax.psum_scatter(x, "tensor", scatter_dimension=1, tiled=True).astype(jnp.float32)
+
+    def finish(*after):
+        arrived = tie(far, *after) if after else far
+        far_near = swap(arrived, "tensor", 1)
+        if twisted():
+            return jnp.concatenate([x, near, arrived, far_near], 1)
+        core, chip = me % 2, me // 2
+        return ordered(chip, ordered(core, x, near), ordered(core, arrived, far_near))
+
+    return finish, far
+
+
+def scatter_cores(x, me):
     f32 = jnp.float32
     core, chip = me % 2, me // 2
     quarter = x.shape[1] // 4
@@ -56,11 +81,17 @@
     own = jnp.where(core == 0, even, odd).astype(f32) + got.astype(f32)
     rows = x.shape[0]
     low, high = own[:rows], own[rows:]
-    got = swap(jnp.where(chip == 0, high, low).astype(x.dtype), "tensor", 2)
-    return jnp.where(chip == 0, low, high) + got.astype(f32)
-
-
-def scatter_tm(x, position):
+    return jnp.where(chip == 0, low, high), jnp.where(chip == 0, high, low).astype(x.dtype)
+
+
+def scatter_tensor(x, me):
+    if lax.axis_size("tensor") != 4:
+        return lax.psum_scatter(x, "tensor", scatter_dimension=1, tiled=True).astype(jnp.float32), x
+    keep, give = scatter_cores(x, me)
+    return keep + swap(give, "tensor", 2).astype(jnp.float32), give
+
+
+def scatter_tm(x, position, twist=0):
     f32 = jnp.float32
     size = lax.axis_size("tm")
     outer = size // 2
@@ -72,7 +103,7 @@
     acc = (keep.astype(f32) + swap(give, "tm", 1).astype(f32)).astype(x.dtype)
 
     def chunk(index):
-        return lax.dynamic_index_in_dim(acc, jnp.clip(index, 0, outer - 1), 0, keepdims=False)
+        return lax.dynamic_index_in_dim(acc, jnp.clip(index, 0, outer - 1) ^ twist, 0, keepdims=False)
 
     right = left = None
     for step in range(outer - 1):
@@ -152,7 +183,7 @@
         out_shape=[shape] * outputs,
         compiler_params=pltpu.CompilerParams(vmem_limit_bytes=40 * 1024 * 1024),
         cost_estimate=pl.CostEstimate(
-            flops=2 * work * rows * rows * width,
+            flops=8 * work * rows * rows * width,
             bytes_accessed=2 * rows * width * (len(arrays) + outputs),
             transcendentals=2 * rows * rows * (width // HD),
         ),
@@ -187,19 +218,32 @@
     me = lax.axis_index("tensor")
     none = jnp.zeros((1,), jnp.int32)
     cuts = [none] * (pairs - 1) + [is_last.astype(jnp.int32).reshape(1)]
-    feats = [
+    twist = me if twisted() else 0
+    row_query, row_key, row_value = (twist_rows(w, me) for w in (w_query, w_key, w_value))
+    started = [
         gather_tensor(frames[index * span : (index + 1) * span], me) for index in range(pairs)
     ]
-    keys = [mm(feat, w_key).astype(bf16) for feat in feats[:1]]
-    values = [mm(feat, w_value).astype(bf16) for feat in feats[:1]]
-    ahead = from_behind(jnp.concatenate([keys[0], values[0]], 1), "tm", -1)
-    keys += [mm(feat, w_key).astype(bf16) for feat in feats[1:]] + [ahead[:, :width]]
-    values += [mm(feat, w_value).astype(bf16) for feat in feats[1:]] + [ahead[:, width:]]
-    queries = [mm(feat, w_query).astype(bf16) for feat in feats]
-    late_grad, _ = lax.optimization_barrier((out_grad, feats[-1]))
+    feats, queries, keys, values = [], [], [], []
+    ready = ()
+    for index in range(pairs):
+        feat = started[index][0](*ready)
+        keys.append(mm(feat, row_key).astype(bf16))
+        values.append(mm(feat, row_value).astype(bf16))
+        queries.append(mm(feat, row_query).astype(bf16))
+        if index == 0:
+            first = jnp.concatenate([keys[0], values[0]], 1)
+            ahead = from_behind(first, "tm", -1)
+        ready = (first, queries[index])
+        feats.append(feat)
+    keys.append(ahead[:, :width])
+    values.append(ahead[:, width:])
+    late_grad = tie(out_grad, started[-1][1])
     all_out_grad = lax.all_gather(late_grad, "tensor", axis=1, tiled=True)
     attended, mixed = [], []
+    given = None
     for index in range(pairs):
+        if given is not None:
+            queries[index] = tie(queries[index], given)
         (heads_out,) = attention(
             forward_kernel,
             1,
@@ -211,7 +255,7 @@
             values[index + 1],
         )
         attended.append(heads_out)
-        summed = scatter_tensor(mm(heads_out, w_out).astype(bf16), me)
+        summed, given = scatter_tensor(mm(heads_out, w_out).astype(bf16), me)
         own = frames[index * span : (index + 1) * span].astype(f32)
         mixed.append((own + summed).astype(bf16))
     mixed = jnp.concatenate(mixed, 0)
@@ -262,14 +306,17 @@
         .reshape(rows, full_width)
         .astype(bf16)
     )
-    attended_grad = mm(piece, w_out, NT).astype(bf16)
+    out_product = mm(piece, attended, TN).astype(bf16)
+    attended_grad = mm(tie(piece, out_product), w_out, NT).astype(bf16)
     grads = [None] * pairs
+    sent = None
     for index in reversed(range(pairs)):
+        asked = queries[index] if sent is None else tie(queries[index], sent)
         grads[index] = attention(
             backward_kernel,
             5,
             cuts[index],
-            queries[index],
+            asked,
             keys[index],
             keys[index + 1],
             values[index],
@@ -277,8 +324,9 @@
             attended_grad[index * span : (index + 1) * span],
         )
         if index == pairs - 1:
-            passed = from_behind(jnp.concatenate([grads[index][2], grads[index][4]], 1), "tm", 1)
-    grad_out = scatter_tm(mm(piece, attended, TN).astype(bf16), position).T
+            sent = jnp.concatenate([grads[index][2], grads[index][4]], 1)
+            passed = from_behind(sent, "tm", 1)
+    grad_out = scatter_tm(out_product, position).T
     small = lax.psum(
         jnp.concatenate([reward_part, term_part[:, None], gain_part[:, None]], 1).astype(bf16),
         "tm",
@@ -289,7 +337,7 @@
         small[:, bins_count + 1],
     )
     query_grad = jnp.concatenate([grad[0] for grad in grads], 0)
-    grad_query = scatter_tm(mm(gathered, query_grad, TN).astype(bf16), position)
+    grad_query = scatter_tm(mm(gathered, query_grad, TN).astype(bf16), position, twist)
 
     def joined(first, second, behind):
         late = [behind] + [grad[second] for grad in grads[:-1]]
@@ -302,9 +350,9 @@
         )
 
     value_grad = joined(3, 4, passed[:, width:])
-    grad_value = scatter_tm(mm(gathered, value_grad, TN).astype(bf16), position)
+    grad_value = scatter_tm(mm(gathered, value_grad, TN).astype(bf16), position, twist)
     key_grad = joined(1, 2, passed[:, :width])
-    grad_key = scatter_tm(mm(gathered, key_grad, TN).astype(bf16), position)
+    grad_key = scatter_tm(mm(gathered, key_grad, TN).astype(bf16), position, twist)
     return (
         mixed,
         pair_losses,

time: 471 us -> 467 us (level)
  waiting for transfers between devices: 188 us -> 166 us
  matrix products: 40 us -> 57 us
    ppermute x2, waiting for transfers between devices: 49.9 us -> 20.9 us  [from_behind(): return lax.ppermute(x, axis, pairs)]
    dot_general x13, matrix products: 35.3 us -> 52.3 us  [mm(): lax.dot_general(left, right, dims, preferred_element_type=jnp.float32)]
    concatenate x2, other arithmetic: 2.25 us -> 14.7 us  [the longest x1 13.5 us: local(): gathered = jnp.concatenate(feats, 0)]
    ppermute x12, waiting for transfers between devices: 19.2 us -> 28.3 us  [scatter_tm(): lax.ppermute(send_right, 'tm', [(2 * a + s, 2 * b + s) for a, b in to_rig...]
    select_n x8 -> x2, other arithmetic: 11.2 us -> 3.1 us  [scatter_cores(): got = swap(jnp.where(core == 0, odd, even), 'tensor', 1)]
    unnamed x109 -> x158, local copies, waits for them, and re-layouts: 15.2 us -> 10.9 us
  transfers between devices with their start and end apart: 42 -> 42, of which waited for: 15 -> 17; matrix products, arithmetic and copies ran while one was open for 21% -> 26% of each run, Pallas kernels for 7% -> 6%
where the time goes in v2:
time: 467 us; the launch traced here: 458 us
  waiting for transfers between devices  166 us (36%)
  starting transfers between devices  87.9 us (19%)
  matrix products  57 us (12%)
  other arithmetic  53.6 us (11%)
  Pallas kernels  33.8 us (7%)
  local copies, waits for them, and re-layouts  31.4 us (7%)
  between operations  17.8 us (4%)
  blocking collectives  11.1 us (2%)
    ppermute x14, waiting for transfers between devices, swap(): lax.ppermute(x, axis, [(i, i ^ bit) for i in range(lax.axis_size(axis))])  105 us
    ppermute x12, starting transfers between devices, scatter_tm(): lax.ppermute(send_right, 'tm', [(2 * a + s, 2 * b + s) for a, b in to_rig...  58.1 us
    dot_general x13, matrix products, mm(): lax.dot_general(left, right, dims, preferred_element_type=jnp.float32)  52.3 us
    pallas_call x4, Pallas kernels, attention(): pl.pallas_call(kernel, grid=(width // HD,), in_specs=[pl.BlockSpec(memory...  33.8 us
    ppermute x12, waiting for transfers between devices, scatter_tm(): lax.ppermute(send_right, 'tm', [(2 * a + s, 2 * b + s) for a, b in to_rig...  28.3 us
    ppermute x2, waiting for transfers between devices, from_behind(): return lax.ppermute(x, axis, pairs)  20.9 us
    concatenate x1, other arithmetic, local(): gathered = jnp.concatenate(feats, 0)  13.5 us
    ppermute x12, starting transfers between devices, scatter_tm(): lax.ppermute(send_left, 'tm', [(2 * a + s, 2 * b + s) for a, b in to_left...  11.8 us
  transfers between devices with their start and end apart: 42, of which 17 were waited for; matrix products, arithmetic and copies ran while one was open for 26% of the time, Pallas kernels for 6%

profile of v2, /device:TPU:0, one launch (start us, length us, event | category | flops | bytes accessed | tf_op | source)
XLA Modules:
  0.0 458.4 jit_solution(7896630240258639231)
XLA Ops:
  8.1 2.8 fusion.71
  10.8 3.0 collective-permute-start.1
  13.8 17.9 %collective-permute-done.1 = bf16[512,768]{1,0:T(8,128)(2,1)} collective-permute-done((bf16[512,768]{1,0:T(8,128)(2,1)}, bf16[512,768]{1,0:T(8,128)(2,1)}, u32[]{:S(2)}, u32[]{:S(2)}) %collective-permute-start.1) | collective-permute-done | bytes 786464 | tf_op jit(solution)/shard_map/ppermute | solution.py:25
  38.1 5.9 %convolution_convert_fusion.11.ka_ref = bf16[512,512]{1,0:T(8,128)(2,1)S(1)} fusion(bf16[768,512]{1,0:T(8,128)(2,1)S(1)} %get-tuple-element.124, bf16[768,512]{1,0:T(8,128)(2,1)S(1)} %get-tuple-element.123, bf16[768,512]{1,0:T(8,128)(2,1)S(1)} %get-tuple-element.125, bf16[768,512]{1,0:T(8,128)(2,1)S(1)} %get-tuple-element.126, ...), kind=kOutput, calls=%fused_computation.44 | convolution fusion | flops 1636040704 | bytes 6815744 | tf_op jit(solution)/shard_map/dot_general | solution.py:15
  44.0 3.8 convolution_convert_fusion.10.va_ref
  49.0 4.4 convolution_convert_fusion.12.q_ref
  56.1 4.6 convolution_convert_fusion.9.kb_ref.ka_ref
  60.7 3.8 convolution_convert_fusion.8.vb_ref.va_ref
  64.6 7.1 %shard_map.178 = bf16[512,512]{1,0:T(8,128)(2,1)S(1)} custom-call(s32[1]{0:T(128)} %constant.176.clone.1.cut_ref, bf16[512,512]{1,0:T(8,128)(2,1)S(1)} %copy-done.16, bf16[512,512]{1,0:T(8,128)(2,1)S(1)} %copy-done.3, bf16[512,512]{1,0:T(8,128)(2,1)S(1)} %convolution_convert_fusion.9.kb_ref.ka_ref, bf16[512,512]{1,0:T(8,128)(2,1)S(1)} %copy-done.6, ...), custom_call_target="tpu_custom_call" | custom-call | flops 4294967296 | bytes 3145728 | tf_op jit(solution)/shard_map/pallas_call | solution.py:178
  78.4 4.7 %convolution_convert_fusion.7.q_ref = bf16[512,512]{1,0:T(8,128)(2,1)S(1)} fusion(bf16[768,512]{1,0:T(8,128)(2,1)} %copy-done.54, bf16[768,512]{1,0:T(8,128)(2,1)} %copy-done.55, bf16[768,512]{1,0:T(8,128)(2,1)} %copy-done.53, bf16[768,512]{1,0:T(8,128)(2,1)} %copy-done.52, bf16[512,768]{1,0:T(8,128)(2,1)} %collective-permute-done.5, ...), kind=kOutput, calls=%fused_computation.40 | convolution fusion | flops 1636040704 | bytes 6815744 | tf_op jit(solution)/shard_map/dot_general | solution.py:15
  83.1 20.9 %collective-permute-done.8 = bf16[512,1024]{1,0:T(8,128)(2,1)} collective-permute-done((bf16[512,1024]{1,0:T(8,128)(2,1)}, bf16[512,1024]{1,0:T(8,128)(2,1)}, u32[]{:S(2)}, u32[]{:S(2)}) %collective-permute-start.8) | collective-permute-done | bytes 1048608 | tf_op jit(solution)/shard_map/ppermute | solution.py:21
  109.7 7.1 %shard_map.179 = bf16[512,512]{1,0:T(8,128)(2,1)S(1)} custom-call(s32[1]{0:T(128)} %bitcast.cut_ref, bf16[512,512]{1,0:T(8,128)(2,1)S(1)} %convolution_convert_fusion.7.q_ref, bf16[512,512]{1,0:T(8,128)(2,1)S(1)} %copy-done.19, bf16[512,512]{1,0:T(8,128)(2,1)S(1)} %get-tuple-element.118.kb_ref, bf16[512,512]{1,0:T(8,128)(2,1)S(1)} %copy-done.22, ...), custom_call_target="tpu_custom_call" | custom-call | flops 4294967296 | bytes 3145728 | tf_op jit(solution)/shard_map/pallas_call | solution.py:178
  121.9 3.2 collective-permute-done.9
  125.1 2.9 convert_add_fusion.4
  128.5 13.5 %maximum_maximum_fusion = bf16[1024,3072]{1,0:T(8,128)(2,1)} fusion(bf16[512,768]{1,0:T(8,128)(2,1)} %collective-permute-done.5, bf16[512,768]{1,0:T(8,128)(2,1)} %collective-permute-done.4, bf16[512,768]{1,0:T(8,128)(2,1)} %collective-permute-done.3, bf16[512,768]{1,0:T(8,128)(2,1)} %get-tuple-element.112, bf16[512,768]{1,0:T(8,128)(2,1)} %collective-permute-done.2, ...), kind=kLoop, calls=%fused_computation.2 | loop fusion | flops 50331648 | bytes 12582912 | tf_op jit(solution)/shard_map/concatenate | solution.py:263
  142.2 16.6 %collective-permute-done.10 = bf16[512,768]{1,0:T(8,128)(2,1)S(1)} collective-permute-done((bf16[512,768]{1,0:T(8,128)(2,1)S(1)}, bf16[512,768]{1,0:T(8,128)(2,1)S(1)}, u32[]{:S(2)}, u32[]{:S(2)}) %collective-permute-start.10) | collective-permute-done | bytes 786464 | tf_op jit(solution)/shard_map/ppermute | solution.py:25
  163.0 5.7 %psum.14 = f32[2,257]{1,0:T(2,128)S(1)} all-reduce(f32[2,257]{1,0:T(2,128)S(1)} %pad_maximum_fusion.18), channel_id=1, replica_groups=mesh['tm'=8,'tensor'=4] {'tensor'}, use_global_device_ids=true, to_apply=%region_2.3 | all-reduce | flops 514 | bytes 4112 | tf_op jit(solution)/shard_map/psum | solution.py:269
  171.7 5.4 %all_gather.7 = f32[2,3072]{1,0:T(2,128)S(1)} all-gather(f32[2,768]{1,0:T(2,128)S(1)} %get-tuple-element.120), channel_id=1, replica_groups=mesh['tm'=8,'tensor'=4] {'tensor'}, dimensions={1}, use_global_device_ids=true | all-gather | bytes 30720 | tf_op jit(solution)/shard_map/all_gather | solution.py:300
  178.8 4.5 fusion
  183.3 3.7 convolution_convert_fusion.3
  187.1 3.4 convolution_convert_fusion.6
  190.7 9.8 %shard_map.180 = (bf16[512,512]{1,0:T(8,128)(2,1)S(1)}, bf16[512,512]{1,0:T(8,128)(2,1)S(1)}, bf16[512,512]{1,0:T(8,128)(2,1)S(1)}, bf16[512,512]{1,0:T(8,128)(2,1)S(1)}, bf16[512,512]{1,0:T(8,128)(2,1)S(1)}) custom-call(s32[1]{0:T(128)} %bitcast.cut_ref, bf16[512,512]{1,0:T(8,128)(2,1)S(1)} %copy-done.25, bf16[512,512]{1,0:T(8,128)(2,1)S(1)} %copy-done.20, ...), custom_call_target="tpu_custom_call" | custom-call | flops 10737418240 | bytes 5767168 | tf_op jit(solution)/shard_map/pallas_call | solution.py:178
  202.3 5.2 %collective-permute-start.18 = (bf16[512,1024]{1,0:T(8,128)(2,1)}, bf16[512,1024]{1,0:T(8,128)(2,1)}, u32[]{:S(2)}, u32[]{:S(2)}) collective-permute-start(bf16[512,1024]{1,0:T(8,128)(2,1)} %constant_dynamic-update-slice_fusion), channel_id=1, source_target_pairs={{0,4},{4,8},{8,12},{12,16},{16,20},{20,24},{24,28},{1,5},{5,9},{9,... | collective-permute-start | bytes 3145736 | tf_op jit(solution)/shard_map/ppermute | solution.py:21
  207.6 9.8 %shard_map.181 = (bf16[512,512]{1,0:T(8,128)(2,1)S(1)}, bf16[512,512]{1,0:T(8,128)(2,1)S(1)}, bf16[512,512]{1,0:T(8,128)(2,1)S(1)}, bf16[512,512]{1,0:T(8,128)(2,1)S(1)}, bf16[512,512]{1,0:T(8,128)(2,1)S(1)}) custom-call(s32[1]{0:T(128)} %constant.176.clone.1.cut_ref, bf16[512,512]{1,0:T(8,128)(2,1)S(1)} %copy-done.17, bf16[512,512]{1,0:T(8,128)(2,1)S(1)} %copy-done.4, ...), custom_call_target="tpu_custom_call" | custom-call | flops 10737418240 | bytes 5767168 | tf_op jit(solution)/shard_map/pallas_call | solution.py:178
  217.5 3.8 convolution_convert_fusion.2
  224.7 2.6 copy.38
  229.3 2.6 copy.45
  233.9 6.8 %convolution_convert_fusion.1 = bf16[3072,512]{1,0:T(8,128)(2,1)S(1)} fusion(bf16[1024,3072]{1,0:T(8,128)(2,1)} %maximum_maximum_fusion, bf16[512,512]{1,0:T(8,128)(2,1)S(1)} %add_convert_fusion.4, bf16[512,512]{1,0:T(8,128)(2,1)S(1)} %get-tuple-element.114), kind=kOutput, calls=%fused_computation.4 | convolution fusion | flops 3224895488 | bytes 10485760 | tf_op jit(solution)/shard_map/dot_general | solution.py:15
  243.4 3.8 convolution_convert_fusion
  247.2 19.2 %collective-permute-done.11 = bf16[4,384,512]{2,1,0:T(8,128)(2,1)} collective-permute-done((bf16[4,384,512]{2,1,0:T(8,128)(2,1)}, bf16[4,384,512]{2,1,0:T(8,128)(2,1)}, u32[]{:S(2)}, u32[]{:S(2)}) %collective-permute-start.11) | collective-permute-done | bytes 1572896 | tf_op jit(solution)/shard_map/ppermute | solution.py:25
  268.3 4.7 %collective-permute-start.12 = (bf16[384,512]{1,0:T(8,128)(2,1)S(1)}, bf16[384,512]{1,0:T(8,128)(2,1)S(1)}, u32[]{:S(2)}, u32[]{:S(2)}) collective-permute-start(bf16[384,512]{1,0:T(8,128)(2,1)S(1)} %get-tuple-element.107), channel_id=1, source_target_pairs={{0,8},{4,12},{1,9},{5,13},{2,10},{6,14},{3,11},{7,15}} | collective-permute-start | bytes 1179656 | tf_op jit(solution)/shard_map/ppermute | solution.py:118
  273.0 27.1 %collective-permute-done.33 = bf16[4,384,512]{1,2,0:T(8,128)(2,1)} collective-permute-done((bf16[4,384,512]{1,2,0:T(8,128)(2,1)}, bf16[4,384,512]{1,2,0:T(8,128)(2,1)}, u32[]{:S(2)}, u32[]{:S(2)}) %collective-permute-start.33) | collective-permute-done | bytes 1572896 | tf_op jit(solution)/shard_map/ppermute | solution.py:25
  302.7 4.7 %collective-permute-start.34 = (bf16[384,512]{0,1:T(8,128)(2,1)S(1)}, bf16[384,512]{0,1:T(8,128)(2,1)S(1)}, u32[]{:S(2)}, u32[]{:S(2)}) collective-permute-start(bf16[384,512]{0,1:T(8,128)(2,1)S(1)} %get-tuple-element.95), channel_id=1, source_target_pairs={{0,8},{4,12},{1,9},{5,13},{2,10},{6,14},{3,11},{7,15}} | collective-permute-start | bytes 1179656 | tf_op jit(solution)/shard_map/ppermute | solution.py:118
  312.9 2.9 collective-permute-done.34
  315.8 5.1 %collective-permute-start.13 = (bf16[384,512]{1,0:T(8,128)(2,1)}, bf16[384,512]{1,0:T(8,128)(2,1)}, u32[]{:S(2)}, u32[]{:S(2)}) collective-permute-start(bf16[384,512]{1,0:T(8,128)(2,1)} %fusion.36), channel_id=1, source_target_pairs={{0,8},{4,12},{8,16},{12,20},{1,9},{5,13},{9,17},{13,21},{2,10},{6,... | collective-permute-start | bytes 1179656 | tf_op jit(solution)/shard_map/ppermute | solution.py:118
  332.7 4.8 %collective-permute-start.14 = (bf16[384,512]{1,0:T(8,128)(2,1)S(1)}, bf16[384,512]{1,0:T(8,128)(2,1)S(1)}, u32[]{:S(2)}, u32[]{:S(2)}) collective-permute-start(bf16[384,512]{1,0:T(8,128)(2,1)S(1)} %get-tuple-element.105), channel_id=1, source_target_pairs={{0,8},{4,12},{8,16},{12,20},{16,24},{20,28},{1,9},{5,13},{9,17},{1... | collective-permute-start | bytes 1179656 | tf_op jit(solution)/shard_map/ppermute | solution.py:118
  342.7 5.1 %collective-permute-start.20 = (bf16[384,512]{1,0:T(8,128)(2,1)S(1)}, bf16[384,512]{1,0:T(8,128)(2,1)S(1)}, u32[]{:S(2)}, u32[]{:S(2)}) collective-permute-start(bf16[384,512]{1,0:T(8,128)(2,1)S(1)} %get-tuple-element.103), channel_id=1, source_target_pairs={{0,8},{4,12},{1,9},{5,13},{2,10},{6,14},{3,11},{7,15}} | collective-permute-start | bytes 1179656 | tf_op jit(solution)/shard_map/ppermute | solution.py:118
  347.8 19.1 %collective-permute-done.26 = bf16[4,384,512]{2,1,0:T(8,128)(2,1)} collective-permute-done((bf16[4,384,512]{2,1,0:T(8,128)(2,1)}, bf16[4,384,512]{2,1,0:T(8,128)(2,1)}, u32[]{:S(2)}, u32[]{:S(2)}) %collective-permute-start.26) | collective-permute-done | bytes 1572896 | tf_op jit(solution)/shard_map/ppermute | solution.py:25
  369.5 5.2 %collective-permute-start.27 = (bf16[384,512]{1,0:T(8,128)(2,1)S(1)}, bf16[384,512]{1,0:T(8,128)(2,1)S(1)}, u32[]{:S(2)}, u32[]{:S(2)}) collective-permute-start(bf16[384,512]{1,0:T(8,128)(2,1)S(1)} %get-tuple-element.99), channel_id=1, source_target_pairs={{0,8},{4,12},{1,9},{5,13},{2,10},{6,14},{3,11},{7,15}} | collective-permute-start | bytes 1179656 | tf_op jit(solution)/shard_map/ppermute | solution.py:118
  375.6 7.6 %collective-permute-done.27 = bf16[384,512]{1,0:T(8,128)(2,1)S(1)} collective-permute-done((bf16[384,512]{1,0:T(8,128)(2,1)S(1)}, bf16[384,512]{1,0:T(8,128)(2,1)S(1)}, u32[]{:S(2)}, u32[]{:S(2)}) %collective-permute-start.27) | collective-permute-done | bytes 393248 | tf_op jit(solution)/shard_map/ppermute | solution.py:118
  383.3 4.4 collective-permute-start.21
  391.8 5.4 %collective-permute-done.21 = bf16[384,512]{1,0:T(8,128)(2,1)S(1)} collective-permute-done((bf16[384,512]{1,0:T(8,128)(2,1)S(1)}, bf16[384,512]{1,0:T(8,128)(2,1)S(1)}, u32[]{:S(2)}, u32[]{:S(2)}) %collective-permute-start.21) | collective-permute-done | bytes 393248 | tf_op jit(solution)/shard_map/ppermute | solution.py:118
  400.0 5.6 %collective-permute-done.28 = bf16[384,512]{1,0:T(8,128)(2,1)S(1)} collective-permute-done((bf16[384,512]{1,0:T(8,128)(2,1)S(1)}, bf16[384,512]{1,0:T(8,128)(2,1)S(1)}, u32[]{:S(2)}, u32[]{:S(2)}) %collective-permute-start.28) | collective-permute-done | bytes 393248 | tf_op jit(solution)/shard_map/ppermute | solution.py:118
  406.5 5.7 %collective-permute-done.36 = bf16[384,512]{0,1:T(8,128)(2,1)S(1)} collective-permute-done((bf16[384,512]{0,1:T(8,128)(2,1)S(1)}, bf16[384,512]{0,1:T(8,128)(2,1)S(1)}, u32[]{:S(2)}, u32[]{:S(2)}) %collective-permute-start.36) | collective-permute-done | bytes 393248 | tf_op jit(solution)/shard_map/ppermute | solution.py:118
  413.9 5.0 %collective-permute-start.22 = (bf16[384,512]{1,0:T(8,128)(2,1)S(1)}, bf16[384,512]{1,0:T(8,128)(2,1)S(1)}, u32[]{:S(2)}, u32[]{:S(2)}) collective-permute-start(bf16[384,512]{1,0:T(8,128)(2,1)S(1)} %get-tuple-element.101), channel_id=1, source_target_pairs={{0,8},{4,12},{8,16},{12,20},{16,24},{20,28},{1,9},{5,13},{9,17},{1... | collective-permute-start | bytes 1179656 | tf_op jit(solution)/shard_map/ppermute | solution.py:118
  418.9 13.1 %collective-permute-start.29 = (bf16[384,512]{1,0:T(8,128)(2,1)S(1)}, bf16[384,512]{1,0:T(8,128)(2,1)S(1)}, u32[]{:S(2)}, u32[]{:S(2)}) collective-permute-start(bf16[384,512]{1,0:T(8,128)(2,1)S(1)} %get-tuple-element.97), channel_id=1, source_target_pairs={{0,8},{4,12},{8,16},{12,20},{16,24},{20,28},{1,9},{5,13},{9,17},{1... | collective-permute-start | bytes 1179656 | tf_op jit(solution)/shard_map/ppermute | solution.py:118
  437.2 8.0 %collective-permute-done.25 = bf16[384,512]{1,0:T(8,128)(2,1)S(1)} collective-permute-done((bf16[384,512]{1,0:T(8,128)(2,1)S(1)}, bf16[384,512]{1,0:T(8,128)(2,1)S(1)}, u32[]{:S(2)}, u32[]{:S(2)}) %collective-permute-start.25) | collective-permute-done | bytes 393248 | tf_op jit(solution)/shard_map/ppermute | solution.py:121
  446.3 3.2 collective-permute-done.32
  (293 shorter events, 95.7 us)
Async XLA Ops:
  8.0 63.7 %copy-start = (bf16[512,3072]{1,0:T(8,128)(2,1)S(1)}, bf16[512,3072]{1,0:T(8,128)(2,1)}, u32[]{:S(2)}) copy-start(bf16[512,3072]{1,0:T(8,128)(2,1)} %param.15) | copy-start | bytes 9437188
  8.0 170.8 %all-gather.2.cloned.1.call-start = ((), (), s32[]{:S(2)}) async-start(), calls=%async_computation | async-start | bytes 7864320 | tf_op jit(solution)/shard_map/all_gather | solution.py:241
  10.8 20.8 %collective-permute-start.1 = (bf16[512,768]{1,0:T(8,128)(2,1)}, bf16[512,768]{1,0:T(8,128)(2,1)}, u32[]{:S(2)}, u32[]{:S(2)}) collective-permute-start(bf16[512,768]{1,0:T(8,128)(2,1)} %get-tuple-element.111), channel_id=1, source_target_pairs={{0,2},{1,3},{2,0},{3,1},{4,6},{5,7},{6,4},{7,5},{8,10},{9,11},{10,... | collective-permute-start | bytes 2359304 | tf_op jit(solution)/shard_map/ppermute | solution.py:25
  13.8 24.2 %collective-permute-start = (bf16[512,768]{1,0:T(8,128)(2,1)}, bf16[512,768]{1,0:T(8,128)(2,1)}, u32[]{:S(2)}, u32[]{:S(2)}) collective-permute-start(bf16[512,768]{1,0:T(8,128)(2,1)} %get-tuple-element.111), channel_id=1, source_target_pairs={{0,1},{1,0},{2,3},{3,2},{4,5},{5,4},{6,7},{7,6},{8,9},{9,8},{10,11... | collective-permute-start | bytes 2359304 | tf_op jit(solution)/shard_map/ppermute | solution.py:25
  31.7 6.4 %collective-permute-start.2 = (bf16[512,768]{1,0:T(8,128)(2,1)}, bf16[512,768]{1,0:T(8,128)(2,1)}, u32[]{:S(2)}, u32[]{:S(2)}) collective-permute-start(bf16[512,768]{1,0:T(8,128)(2,1)} %collective-permute-done.1), channel_id=1, source_target_pairs={{0,1},{1,0},{2,3},{3,2},{4,5},{5,4},{6,7},{7,6},{8,9},{9,8},{10,11... | collective-permute-start | bytes 2359304 | tf_op jit(solution)/shard_map/ppermute | solution.py:25
  31.7 21.8 %collective-permute-start.4 = (bf16[512,768]{1,0:T(8,128)(2,1)}, bf16[512,768]{1,0:T(8,128)(2,1)}, u32[]{:S(2)}, u32[]{:S(2)}) collective-permute-start(bf16[512,768]{1,0:T(8,128)(2,1)} %get-tuple-element.112), channel_id=1, source_target_pairs={{0,2},{1,3},{2,0},{3,1},{4,6},{5,7},{6,4},{7,5},{8,10},{9,11},{10,... | collective-permute-start | bytes 2359304 | tf_op jit(solution)/shard_map/ppermute | solution.py:25
  33.4 20.4 %collective-permute-start.3 = (bf16[512,768]{1,0:T(8,128)(2,1)}, bf16[512,768]{1,0:T(8,128)(2,1)}, u32[]{:S(2)}, u32[]{:S(2)}) collective-permute-start(bf16[512,768]{1,0:T(8,128)(2,1)} %get-tuple-element.112), channel_id=1, source_target_pairs={{0,1},{1,0},{2,3},{3,2},{4,5},{5,4},{6,7},{7,6},{8,9},{9,8},{10,11... | collective-permute-start | bytes 2359304 | tf_op jit(solution)/shard_map/ppermute | solution.py:25
  53.5 2.6 collective-permute-start.5
  76.2 29.1 %collective-permute-start.6 = (bf16[1024,768]{1,0:T(8,128)(2,1)}, bf16[1024,768]{1,0:T(8,128)(2,1)}, u32[]{:S(2)}, u32[]{:S(2)}) collective-permute-start(bf16[1024,768]{1,0:T(8,128)(2,1)} %broadcast_select_fusion.1), channel_id=1, source_target_pairs={{0,1},{1,0},{2,3},{3,2},{4,5},{5,4},{6,7},{7,6},{8,9},{9,8},{10,11... | collective-permute-start | bytes 4718600 | tf_op jit(solution)/shard_map/ppermute | solution.py:25
  76.5 27.5 %collective-permute-start.8 = (bf16[512,1024]{1,0:T(8,128)(2,1)}, bf16[512,1024]{1,0:T(8,128)(2,1)}, u32[]{:S(2)}, u32[]{:S(2)}) collective-permute-start(bf16[512,1024]{1,0:T(8,128)(2,1)} %pad_maximum_fusion.10), channel_id=1, source_target_pairs={{4,0},{8,4},{12,8},{16,12},{20,16},{24,20},{28,24},{5,1},{9,5},{13... | collective-permute-start | bytes 3145736 | tf_op jit(solution)/shard_map/ppermute | solution.py:21
  77.8 247.6 %all-reduce.2.cloned.1.call-start = ((), (), s32[]{:S(2)}) async-start(), calls=%async_computation.1 | async-start | bytes 811008 | tf_op jit(solution)/shard_map/psum | solution.py:330
  121.2 3.8 collective-permute-start.9
  121.5 20.7 %collective-permute-start.7 = (bf16[512,768]{1,0:T(8,128)(2,1)}, bf16[512,768]{1,0:T(8,128)(2,1)S(1)}, u32[]{:S(2)}, u32[]{:S(2)}) collective-permute-start(bf16[512,768]{1,0:T(8,128)(2,1)} %select_convert_fusion.1), channel_id=1, source_target_pairs={{0,2},{1,3},{2,0},{3,1},{4,6},{5,7},{6,4},{7,5},{8,10},{9,11},{10,... | collective-permute-start | bytes 2359304 | tf_op jit(solution)/shard_map/ppermute | solution.py:25
  128.1 30.7 %copy-start.27 = (f32[1024,768]{1,0:T(8,128)S(1)}, f32[1024,768]{1,0:T(8,128)}, u32[]{:S(2)}) copy-start(f32[1024,768]{1,0:T(8,128)} %copy-done.26) | copy-start | bytes 9437188
  128.1 30.7 %copy-start.42 = (bf16[1024,768]{1,0:T(8,128)(2,1)S(1)}, bf16[1024,768]{1,0:T(8,128)(2,1)}, u32[]{:S(2)}) copy-start(bf16[1024,768]{1,0:T(8,128)(2,1)} %param.11) | copy-start | bytes 4718596
  128.1 30.6 %collective-permute-start.10 = (bf16[512,768]{1,0:T(8,128)(2,1)S(1)}, bf16[512,768]{1,0:T(8,128)(2,1)S(1)}, u32[]{:S(2)}, u32[]{:S(2)}) collective-permute-start(bf16[512,768]{1,0:T(8,128)(2,1)S(1)} %select_convert_fusion), channel_id=1, source_target_pairs={{0,2},{1,3},{2,0},{3,1},{4,6},{5,7},{6,4},{7,5},{8,10},{9,11},{10,... | collective-permute-start | bytes 2359304 | tf_op jit(solution)/shard_map/ppermute | solution.py:25
  202.3 29.9 %collective-permute-start.18 = (bf16[512,1024]{1,0:T(8,128)(2,1)}, bf16[512,1024]{1,0:T(8,128)(2,1)}, u32[]{:S(2)}, u32[]{:S(2)}) collective-permute-start(bf16[512,1024]{1,0:T(8,128)(2,1)} %constant_dynamic-update-slice_fusion), channel_id=1, source_target_pairs={{0,4},{4,8},{8,12},{12,16},{16,20},{20,24},{24,28},{1,5},{5,9},{9,... | collective-permute-start | bytes 3145736 | tf_op jit(solution)/shard_map/ppermute | solution.py:21
  222.7 43.7 %collective-permute-start.11 = (bf16[4,384,512]{2,1,0:T(8,128)(2,1)}, bf16[4,384,512]{2,1,0:T(8,128)(2,1)}, u32[]{:S(2)}, u32[]{:S(2)}) collective-permute-start(bf16[4,384,512]{2,1,0:T(8,128)(2,1)} %dynamic-slice_bitcast_fusion.2), channel_id=1, source_target_pairs={{0,4},{4,0},{8,12},{12,8},{16,20},{20,16},{24,28},{28,24},{1,5},{5... | collective-permute-start | bytes 4718600 | tf_op jit(solution)/shard_map/ppermute | solution.py:25
  227.3 72.8 %collective-permute-start.33 = (bf16[4,384,512]{1,2,0:T(8,128)(2,1)}, bf16[4,384,512]{1,2,0:T(8,128)(2,1)}, u32[]{:S(2)}, u32[]{:S(2)}) collective-permute-start(bf16[4,384,512]{1,2,0:T(8,128)(2,1)} %bitcast.154), channel_id=1, source_target_pairs={{0,4},{4,0},{8,12},{12,8},{16,20},{20,16},{24,28},{28,24},{1,5},{5... | collective-permute-start | bytes 4718600 | tf_op jit(solution)/shard_map/ppermute | solution.py:25
  242.1 98.6 %collective-permute-start.19 = (bf16[4,384,512]{2,1,0:T(8,128)(2,1)}, bf16[4,384,512]{2,1,0:T(8,128)(2,1)}, u32[]{:S(2)}, u32[]{:S(2)}) collective-permute-start(bf16[4,384,512]{2,1,0:T(8,128)(2,1)} %dynamic-slice_bitcast_fusion.1), channel_id=1, source_target_pairs={{0,4},{4,0},{8,12},{12,8},{16,20},{20,16},{24,28},{28,24},{1,5},{5... | collective-permute-start | bytes 4718600 | tf_op jit(solution)/shard_map/ppermute | solution.py:25
  247.2 60.2 %copy-start.44 = (bf16[3072,512]{1,0:T(8,128)(2,1)}, bf16[3072,512]{1,0:T(8,128)(2,1)S(1)}, u32[]{:S(2)}) copy-start(bf16[3072,512]{1,0:T(8,128)(2,1)S(1)} %convolution_convert_fusion) | copy-start | bytes 9437188
  247.2 52.9 %copy-start.41 = (bf16[4,1,384,512]{2,3,0,1:T(8,128)(2,1)S(1)}, bf16[4,1,384,512]{2,3,0,1:T(8,128)(2,1)}, u32[]{:S(2)}) copy-start(bf16[4,1,384,512]{2,3,0,1:T(8,128)(2,1)} %copy.45) | copy-start | bytes 4718596
  268.2 121.5 %copy-start.28 = (bf16[4,384,512]{2,1,0:T(8,128)(2,1)}, bf16[4,384,512]{2,1,0:T(8,128)(2,1)S(1)}, u32[]{:S(2)}) copy-start(bf16[4,384,512]{2,1,0:T(8,128)(2,1)S(1)} %fusion.4) | copy-start | bytes 4718596
  268.3 42.3 %collective-permute-start.12 = (bf16[384,512]{1,0:T(8,128)(2,1)S(1)}, bf16[384,512]{1,0:T(8,128)(2,1)S(1)}, u32[]{:S(2)}, u32[]{:S(2)}) collective-permute-start(bf16[384,512]{1,0:T(8,128)(2,1)S(1)} %get-tuple-element.107), channel_id=1, source_target_pairs={{0,8},{4,12},{1,9},{5,13},{2,10},{6,14},{3,11},{7,15}} | collective-permute-start | bytes 1179656 | tf_op jit(solution)/shard_map/ppermute | solution.py:118
  302.7 13.1 %collective-permute-start.34 = (bf16[384,512]{0,1:T(8,128)(2,1)S(1)}, bf16[384,512]{0,1:T(8,128)(2,1)S(1)}, u32[]{:S(2)}, u32[]{:S(2)}) collective-permute-start(bf16[384,512]{0,1:T(8,128)(2,1)S(1)} %get-tuple-element.95), channel_id=1, source_target_pairs={{0,8},{4,12},{1,9},{5,13},{2,10},{6,14},{3,11},{7,15}} | collective-permute-start | bytes 1179656 | tf_op jit(solution)/shard_map/ppermute | solution.py:118
  308.6 58.2 %collective-permute-start.26 = (bf16[4,384,512]{2,1,0:T(8,128)(2,1)}, bf16[4,384,512]{2,1,0:T(8,128)(2,1)}, u32[]{:S(2)}, u32[]{:S(2)}) collective-permute-start(bf16[4,384,512]{2,1,0:T(8,128)(2,1)} %dynamic-slice_bitcast_fusion), channel_id=1, source_target_pairs={{0,4},{4,0},{8,12},{12,8},{16,20},{20,16},{24,28},{28,24},{1,5},{5... | collective-permute-start | bytes 4718600 | tf_op jit(solution)/shard_map/ppermute | solution.py:25
  309.9 11.9 %collective-permute-start.15 = (bf16[384,512]{1,0:T(8,128)(2,1)S(1)}, bf16[384,512]{1,0:T(8,128)(2,1)S(1)}, u32[]{:S(2)}, u32[]{:S(2)}) collective-permute-start(bf16[384,512]{1,0:T(8,128)(2,1)S(1)} %get-tuple-element.108), channel_id=1, source_target_pairs={{24,16},{28,20},{25,17},{29,21},{26,18},{30,22},{27,19},{31,23}} | collective-permute-start | bytes 1179656 | tf_op jit(solution)/shard_map/ppermute | solution.py:121
  310.6 22.0 %collective-permute-start.37 = (bf16[384,512]{0,1:T(8,128)(2,1)}, bf16[384,512]{0,1:T(8,128)(2,1)}, u32[]{:S(2)}, u32[]{:S(2)}) collective-permute-start(bf16[384,512]{0,1:T(8,128)(2,1)} %get-tuple-element.96), channel_id=1, source_target_pairs={{24,16},{28,20},{25,17},{29,21},{26,18},{30,22},{27,19},{31,23}} | collective-permute-start | bytes 1179656 | tf_op jit(solution)/shard_map/ppermute | solution.py:121
  315.8 14.5 %collective-permute-start.13 = (bf16[384,512]{1,0:T(8,128)(2,1)}, bf16[384,512]{1,0:T(8,128)(2,1)}, u32[]{:S(2)}, u32[]{:S(2)}) collective-permute-start(bf16[384,512]{1,0:T(8,128)(2,1)} %fusion.36), channel_id=1, source_target_pairs={{0,8},{4,12},{8,16},{12,20},{1,9},{5,13},{9,17},{13,21},{2,10},{6,... | collective-permute-start | bytes 1179656 | tf_op jit(solution)/shard_map/ppermute | solution.py:118
  322.6 15.9 %collective-permute-start.35 = (bf16[384,512]{0,1:T(8,128)(2,1)}, bf16[384,512]{0,1:T(8,128)(2,1)}, u32[]{:S(2)}, u32[]{:S(2)}) collective-permute-start(bf16[384,512]{0,1:T(8,128)(2,1)} %fusion.20), channel_id=1, source_target_pairs={{0,8},{4,12},{8,16},{12,20},{1,9},{5,13},{9,17},{13,21},{2,10},{6,... | collective-permute-start | bytes 1179656 | tf_op jit(solution)/shard_map/ppermute | solution.py:118
  332.0 55.8 %collective-permute-start.16 = (bf16[384,512]{1,0:T(8,128)(2,1)S(1)}, bf16[384,512]{1,0:T(8,128)(2,1)S(1)}, u32[]{:S(2)}, u32[]{:S(2)}) collective-permute-start(bf16[384,512]{1,0:T(8,128)(2,1)S(1)} %get-tuple-element.106), channel_id=1, source_target_pairs={{24,16},{28,20},{16,8},{20,12},{25,17},{29,21},{17,9},{21,13},{26,... | collective-permute-start | bytes 1179656 | tf_op jit(solution)/shard_map/ppermute | solution.py:121
  332.7 100.9 %collective-permute-start.14 = (bf16[384,512]{1,0:T(8,128)(2,1)S(1)}, bf16[384,512]{1,0:T(8,128)(2,1)S(1)}, u32[]{:S(2)}, u32[]{:S(2)}) collective-permute-start(bf16[384,512]{1,0:T(8,128)(2,1)S(1)} %get-tuple-element.105), channel_id=1, source_target_pairs={{0,8},{4,12},{8,16},{12,20},{16,24},{20,28},{1,9},{5,13},{9,17},{1... | collective-permute-start | bytes 1179656 | tf_op jit(solution)/shard_map/ppermute | solution.py:118
  339.8 29.6 %collective-permute-start.38 = (bf16[384,512]{0,1:T(8,128)(2,1)S(1)}, bf16[384,512]{0,1:T(8,128)(2,1)S(1)}, u32[]{:S(2)}, u32[]{:S(2)}) collective-permute-start(bf16[384,512]{0,1:T(8,128)(2,1)S(1)} %get-tuple-element.94), channel_id=1, source_target_pairs={{24,16},{28,20},{16,8},{20,12},{25,17},{29,21},{17,9},{21,13},{26,... | collective-permute-start | bytes 1179656 | tf_op jit(solution)/shard_map/ppermute | solution.py:121
  342.7 32.1 %collective-permute-start.20 = (bf16[384,512]{1,0:T(8,128)(2,1)S(1)}, bf16[384,512]{1,0:T(8,128)(2,1)S(1)}, u32[]{:S(2)}, u32[]{:S(2)}) collective-permute-start(bf16[384,512]{1,0:T(8,128)(2,1)S(1)} %get-tuple-element.103), channel_id=1, source_target_pairs={{0,8},{4,12},{1,9},{5,13},{2,10},{6,14},{3,11},{7,15}} | collective-permute-start | bytes 1179656 | tf_op jit(solution)/shard_map/ppermute | solution.py:118
  366.9 23.0 %collective-permute-start.23 = (bf16[384,512]{1,0:T(8,128)(2,1)S(1)}, bf16[384,512]{1,0:T(8,128)(2,1)S(1)}, u32[]{:S(2)}, u32[]{:S(2)}) collective-permute-start(bf16[384,512]{1,0:T(8,128)(2,1)S(1)} %get-tuple-element.104), channel_id=1, source_target_pairs={{24,16},{28,20},{25,17},{29,21},{26,18},{30,22},{27,19},{31,23}} | collective-permute-start | bytes 1179656 | tf_op jit(solution)/shard_map/ppermute | solution.py:121
  369.5 13.8 %collective-permute-start.27 = (bf16[384,512]{1,0:T(8,128)(2,1)S(1)}, bf16[384,512]{1,0:T(8,128)(2,1)S(1)}, u32[]{:S(2)}, u32[]{:S(2)}) collective-permute-start(bf16[384,512]{1,0:T(8,128)(2,1)S(1)} %get-tuple-element.99), channel_id=1, source_target_pairs={{0,8},{4,12},{1,9},{5,13},{2,10},{6,14},{3,11},{7,15}} | collective-permute-start | bytes 1179656 | tf_op jit(solution)/shard_map/ppermute | solution.py:118
  374.8 23.9 %collective-permute-start.30 = (bf16[384,512]{1,0:T(8,128)(2,1)S(1)}, bf16[384,512]{1,0:T(8,128)(2,1)S(1)}, u32[]{:S(2)}, u32[]{:S(2)}) collective-permute-start(bf16[384,512]{1,0:T(8,128)(2,1)S(1)} %get-tuple-element.100), channel_id=1, source_target_pairs={{24,16},{28,20},{25,17},{29,21},{26,18},{30,22},{27,19},{31,23}} | collective-permute-start | bytes 1179656 | tf_op jit(solution)/shard_map/ppermute | solution.py:121
  383.3 13.9 %collective-permute-start.21 = (bf16[384,512]{1,0:T(8,128)(2,1)S(1)}, bf16[384,512]{1,0:T(8,128)(2,1)S(1)}, u32[]{:S(2)}, u32[]{:S(2)}) collective-permute-start(bf16[384,512]{1,0:T(8,128)(2,1)S(1)} %fusion.31), channel_id=1, source_target_pairs={{0,8},{4,12},{8,16},{12,20},{1,9},{5,13},{9,17},{13,21},{2,10},{6,... | collective-permute-start | bytes 1179656 | tf_op jit(solution)/shard_map/ppermute | solution.py:118
  387.8 17.8 %collective-permute-start.28 = (bf16[384,512]{1,0:T(8,128)(2,1)S(1)}, bf16[384,512]{1,0:T(8,128)(2,1)S(1)}, u32[]{:S(2)}, u32[]{:S(2)}) collective-permute-start(bf16[384,512]{1,0:T(8,128)(2,1)S(1)} %fusion.26), channel_id=1, source_target_pairs={{0,8},{4,12},{8,16},{12,20},{1,9},{5,13},{9,17},{13,21},{2,10},{6,... | collective-permute-start | bytes 1179656 | tf_op jit(solution)/shard_map/ppermute | solution.py:118
  389.9 22.4 %collective-permute-start.36 = (bf16[384,512]{0,1:T(8,128)(2,1)S(1)}, bf16[384,512]{0,1:T(8,128)(2,1)S(1)}, u32[]{:S(2)}, u32[]{:S(2)}) collective-permute-start(bf16[384,512]{0,1:T(8,128)(2,1)S(1)} %get-tuple-element.93), channel_id=1, source_target_pairs={{0,8},{4,12},{8,16},{12,20},{16,24},{20,28},{1,9},{5,13},{9,17},{1... | collective-permute-start | bytes 1179656 | tf_op jit(solution)/shard_map/ppermute | solution.py:118
  397.2 15.7 %collective-permute-start.39 = (bf16[384,512]{0,1:T(8,128)(2,1)S(1)}, bf16[384,512]{0,1:T(8,128)(2,1)S(1)}, u32[]{:S(2)}, u32[]{:S(2)}) collective-permute-start(bf16[384,512]{0,1:T(8,128)(2,1)S(1)} %fusion.19), channel_id=1, source_target_pairs={{24,16},{28,20},{16,8},{20,12},{8,0},{12,4},{25,17},{29,21},{17,9}... | collective-permute-start | bytes 1179656 | tf_op jit(solution)/shard_map/ppermute | solution.py:121
  398.7 36.4 %collective-permute-start.17 = (bf16[384,512]{1,0:T(8,128)(2,1)S(1)}, bf16[384,512]{1,0:T(8,128)(2,1)S(1)}, u32[]{:S(2)}, u32[]{:S(2)}) collective-permute-start(bf16[384,512]{1,0:T(8,128)(2,1)S(1)} %fusion.35), channel_id=1, source_target_pairs={{24,16},{28,20},{16,8},{20,12},{8,0},{12,4},{25,17},{29,21},{17,9}... | collective-permute-start | bytes 1179656 | tf_op jit(solution)/shard_map/ppermute | solution.py:121
  405.6 13.3 %collective-permute-start.24 = (bf16[384,512]{1,0:T(8,128)(2,1)S(1)}, bf16[384,512]{1,0:T(8,128)(2,1)S(1)}, u32[]{:S(2)}, u32[]{:S(2)}) collective-permute-start(bf16[384,512]{1,0:T(8,128)(2,1)S(1)} %get-tuple-element.102), channel_id=1, source_target_pairs={{24,16},{28,20},{16,8},{20,12},{25,17},{29,21},{17,9},{21,13},{26,... | collective-permute-start | bytes 1179656 | tf_op jit(solution)/shard_map/ppermute | solution.py:121
  412.2 19.9 %collective-permute-start.31 = (bf16[384,512]{1,0:T(8,128)(2,1)S(1)}, bf16[384,512]{1,0:T(8,128)(2,1)S(1)}, u32[]{:S(2)}, u32[]{:S(2)}) collective-permute-start(bf16[384,512]{1,0:T(8,128)(2,1)S(1)} %get-tuple-element.98), channel_id=1, source_target_pairs={{24,16},{28,20},{16,8},{20,12},{25,17},{29,21},{17,9},{21,13},{26,... | collective-permute-start | bytes 1179656 | tf_op jit(solution)/shard_map/ppermute | solution.py:121
  413.9 23.3 %collective-permute-start.22 = (bf16[384,512]{1,0:T(8,128)(2,1)S(1)}, bf16[384,512]{1,0:T(8,128)(2,1)S(1)}, u32[]{:S(2)}, u32[]{:S(2)}) collective-permute-start(bf16[384,512]{1,0:T(8,128)(2,1)S(1)} %get-tuple-element.101), channel_id=1, source_target_pairs={{0,8},{4,12},{8,16},{12,20},{16,24},{20,28},{1,9},{5,13},{9,17},{1... | collective-permute-start | bytes 1179656 | tf_op jit(solution)/shard_map/ppermute | solution.py:118
  418.9 27.3 %collective-permute-start.29 = (bf16[384,512]{1,0:T(8,128)(2,1)S(1)}, bf16[384,512]{1,0:T(8,128)(2,1)S(1)}, u32[]{:S(2)}, u32[]{:S(2)}) collective-permute-start(bf16[384,512]{1,0:T(8,128)(2,1)S(1)} %get-tuple-element.97), channel_id=1, source_target_pairs={{0,8},{4,12},{8,16},{12,20},{16,24},{20,28},{1,9},{5,13},{9,17},{1... | collective-permute-start | bytes 1179656 | tf_op jit(solution)/shard_map/ppermute | solution.py:118
  432.2 13.1 %collective-permute-start.25 = (bf16[384,512]{1,0:T(8,128)(2,1)S(1)}, bf16[384,512]{1,0:T(8,128)(2,1)S(1)}, u32[]{:S(2)}, u32[]{:S(2)}) collective-permute-start(bf16[384,512]{1,0:T(8,128)(2,1)S(1)} %fusion.30), channel_id=1, source_target_pairs={{24,16},{28,20},{16,8},{20,12},{8,0},{12,4},{25,17},{29,21},{17,9}... | collective-permute-start | bytes 1179656 | tf_op jit(solution)/shard_map/ppermute | solution.py:121
  433.6 15.8 %collective-permute-start.32 = (bf16[384,512]{1,0:T(8,128)(2,1)S(1)}, bf16[384,512]{1,0:T(8,128)(2,1)S(1)}, u32[]{:S(2)}, u32[]{:S(2)}) collective-permute-start(bf16[384,512]{1,0:T(8,128)(2,1)S(1)} %fusion.25), channel_id=1, source_target_pairs={{24,16},{28,20},{16,8},{20,12},{8,0},{12,4},{25,17},{29,21},{17,9}... | collective-permute-start | bytes 1179656 | tf_op jit(solution)/shard_map/ppermute | solution.py:121
  (71 other events, 571.4 us)
Sparse Core Ops, SparseCore 0:
  77.9 49.0 all-gather.1
Sparse Core Ops, SparseCore 1:
  178.9 79.2 all-reduce.1

commit v3 on v2

--- a/solution.py
+++ b/solution.py
@@ -91,16 +91,25 @@
     return keep + swap(give, "tensor", 2).astype(jnp.float32), give
 
 
-def scatter_tm(x, position, twist=0):
+def halve_tm(x, position):
+    size = lax.axis_size("tm")
+    rows, width = x.shape
+    x = x.reshape(size // 2, 2, rows // size, width)
+    side = position % 2
+    keep = lax.dynamic_index_in_dim(x, side, 1, keepdims=False)
+    return keep, lax.dynamic_index_in_dim(x, 1 - side, 1, keepdims=False)
+
+
+def scatter_tm(halves, position, twist=0, after=()):
     f32 = jnp.float32
+    keep, give = halves
     size = lax.axis_size("tm")
     outer = size // 2
-    rows, width = x.shape
-    x = x.reshape(outer, 2, rows // size, width)
-    side, place = position % 2, position // 2
-    keep = lax.dynamic_index_in_dim(x, side, 1, keepdims=False)
-    give = lax.dynamic_index_in_dim(x, 1 - side, 1, keepdims=False)
-    acc = (keep.astype(f32) + swap(give, "tm", 1).astype(f32)).astype(x.dtype)
+    place = position // 2
+    got = swap(give, "tm", 1)
+    if after:
+        got = tie(got, *after)
+    acc = (keep.astype(f32) + got.astype(f32)).astype(keep.dtype)
 
     def chunk(index):
         return lax.dynamic_index_in_dim(acc, jnp.clip(index, 0, outer - 1) ^ twist, 0, keepdims=False)
@@ -110,8 +119,8 @@
         reach = outer - 1 - step
         send_right, send_left = chunk(place + reach), chunk(place - reach)
         if right is not None:
-            send_right = (send_right.astype(f32) + right.astype(f32)).astype(x.dtype)
-            send_left = (send_left.astype(f32) + left.astype(f32)).astype(x.dtype)
+            send_right = (send_right.astype(f32) + right.astype(f32)).astype(keep.dtype)
+            send_left = (send_left.astype(f32) + left.astype(f32)).astype(keep.dtype)
         to_right = [(o, o + 1) for o in range(step + 1)]
         to_left = [(outer - 1 - a, outer - 1 - b) for a, b in to_right]
         both = range(2)
@@ -326,7 +335,7 @@
         if index == pairs - 1:
             sent = jnp.concatenate([grads[index][2], grads[index][4]], 1)
             passed = from_behind(sent, "tm", 1)
-    grad_out = scatter_tm(out_product, position).T
+    out_halves = halve_tm(out_product, position)
     small = lax.psum(
         jnp.concatenate([reward_part, term_part[:, None], gain_part[:, None]], 1).astype(bf16),
         "tm",
@@ -337,7 +346,7 @@
         small[:, bins_count + 1],
     )
     query_grad = jnp.concatenate([grad[0] for grad in grads], 0)
-    grad_query = scatter_tm(mm(gathered, query_grad, TN).astype(bf16), position, twist)
+    query_halves = halve_tm(mm(gathered, query_grad, TN).astype(bf16), position)
 
     def joined(first, second, behind):
         late = [behind] + [grad[second] for grad in grads[:-1]]
@@ -350,9 +359,14 @@
         )
 
     value_grad = joined(3, 4, passed[:, width:])
-    grad_value = scatter_tm(mm(gathered, value_grad, TN).astype(bf16), position, twist)
+    value_halves = halve_tm(mm(gathered, value_grad, TN).astype(bf16), position)
     key_grad = joined(1, 2, passed[:, :width])
-    grad_key = scatter_tm(mm(gathered, key_grad, TN).astype(bf16), position, twist)
+    key_halves = halve_tm(mm(gathered, key_grad, TN).astype(bf16), position)
+    gives = (query_halves[1], value_halves[1], key_halves[1])
+    grad_out = scatter_tm(out_halves, position, after=gives).T
+    grad_query = scatter_tm(query_halves, position, twist, after=gives)
+    grad_value = scatter_tm(value_halves, position, twist)
+    grad_key = scatter_tm(key_halves, position, twist)
     return (
         mixed,
         pair_losses,

time: 467 us -> 467 us (level)
  no operation moved by 1% of the time
where the time goes in v3:
time: 467 us; the launch traced here: 458 us
  waiting for transfers between devices  165 us (35%)
  starting transfers between devices  87.8 us (19%)
  matrix products  57 us (12%)
  other arithmetic  53.6 us (11%)
  Pallas kernels  33.7 us (7%)
  local copies, waits for them, and re-layouts  32.5 us (7%)
  between operations  17.8 us (4%)
  blocking collectives  11.1 us (2%)
    ppermute x14, waiting for transfers between devices, swap(): lax.ppermute(x, axis, [(i, i ^ bit) for i in range(lax.axis_size(axis))])  103 us
    ppermute x12, starting transfers between devices, scatter_tm(): lax.ppermute(send_right, 'tm', [(2 * a + s, 2 * b + s) for a, b in to_rig...  58 us
    dot_general x13, matrix products, mm(): lax.dot_general(left, right, dims, preferred_element_type=jnp.float32)  52.3 us
    pallas_call x4, Pallas kernels, attention(): pl.pallas_call(kernel, grid=(width // HD,), in_specs=[pl.BlockSpec(memory...  33.7 us
    ppermute x12, waiting for transfers between devices, scatter_tm(): lax.ppermute(send_right, 'tm', [(2 * a + s, 2 * b + s) for a, b in to_rig...  29.9 us
    ppermute x2, waiting for transfers between devices, from_behind(): return lax.ppermute(x, axis, pairs)  20.9 us
    concatenate x1, other arithmetic, local(): gathered = jnp.concatenate(feats, 0)  13.5 us
    unnamed x158, local copies, waits for them, and re-layouts  12 us
  transfers between devices with their start and end apart: 42, of which 17 were waited for; matrix products, arithmetic and copies ran while one was open for 26% of the time, Pallas kernels for 6%

profile of v3, /device:TPU:0, one launch (start us, length us, event | category | flops | bytes accessed | tf_op | source)
XLA Modules:
  0.0 458.5 jit_solution(6546538467995570606)
XLA Ops:
  8.1 2.8 fusion.71
  10.8 3.0 collective-permute-start.1
  13.8 17.9 %collective-permute-done.1 = bf16[512,768]{1,0:T(8,128)(2,1)} collective-permute-done((bf16[512,768]{1,0:T(8,128)(2,1)}, bf16[512,768]{1,0:T(8,128)(2,1)}, u32[]{:S(2)}, u32[]{:S(2)}) %collective-permute-start.1) | collective-permute-done | bytes 786464 | tf_op jit(solution)/shard_map/ppermute | solution.py:25
  38.1 5.9 %convolution_convert_fusion.11.ka_ref = bf16[512,512]{1,0:T(8,128)(2,1)S(1)} fusion(bf16[768,512]{1,0:T(8,128)(2,1)S(1)} %get-tuple-element.128, bf16[768,512]{1,0:T(8,128)(2,1)S(1)} %get-tuple-element.127, bf16[768,512]{1,0:T(8,128)(2,1)S(1)} %get-tuple-element.129, bf16[768,512]{1,0:T(8,128)(2,1)S(1)} %get-tuple-element.130, ...), kind=kOutput, calls=%fused_computation.44 | convolution fusion | flops 1636040704 | bytes 6815744 | tf_op jit(solution)/shard_map/dot_general | solution.py:15
  44.0 3.8 convolution_convert_fusion.10.va_ref
  49.0 4.4 convolution_convert_fusion.12.q_ref
  56.1 4.6 convolution_convert_fusion.9.kb_ref.ka_ref
  60.7 3.8 convolution_convert_fusion.8.vb_ref.va_ref
  64.6 7.1 %shard_map.178 = bf16[512,512]{1,0:T(8,128)(2,1)S(1)} custom-call(s32[1]{0:T(128)} %constant.176.clone.1.cut_ref, bf16[512,512]{1,0:T(8,128)(2,1)S(1)} %copy-done.16, bf16[512,512]{1,0:T(8,128)(2,1)S(1)} %copy-done.3, bf16[512,512]{1,0:T(8,128)(2,1)S(1)} %convolution_convert_fusion.9.kb_ref.ka_ref, bf16[512,512]{1,0:T(8,128)(2,1)S(1)} %copy-done.6, ...), custom_call_target="tpu_custom_call" | custom-call | flops 4294967296 | bytes 3145728 | tf_op jit(solution)/shard_map/pallas_call | solution.py:187
  78.4 4.7 %convolution_convert_fusion.7.q_ref = bf16[512,512]{1,0:T(8,128)(2,1)S(1)} fusion(bf16[768,512]{1,0:T(8,128)(2,1)} %copy-done.54, bf16[768,512]{1,0:T(8,128)(2,1)} %copy-done.55, bf16[768,512]{1,0:T(8,128)(2,1)} %copy-done.53, bf16[768,512]{1,0:T(8,128)(2,1)} %copy-done.52, bf16[512,768]{1,0:T(8,128)(2,1)} %collective-permute-done.5, ...), kind=kOutput, calls=%fused_computation.40 | convolution fusion | flops 1636040704 | bytes 6815744 | tf_op jit(solution)/shard_map/dot_general | solution.py:15
  83.1 20.9 %collective-permute-done.8 = bf16[512,1024]{1,0:T(8,128)(2,1)} collective-permute-done((bf16[512,1024]{1,0:T(8,128)(2,1)}, bf16[512,1024]{1,0:T(8,128)(2,1)}, u32[]{:S(2)}, u32[]{:S(2)}) %collective-permute-start.8) | collective-permute-done | bytes 1048608 | tf_op jit(solution)/shard_map/ppermute | solution.py:21
  109.7 7.1 %shard_map.179 = bf16[512,512]{1,0:T(8,128)(2,1)S(1)} custom-call(s32[1]{0:T(128)} %bitcast.cut_ref, bf16[512,512]{1,0:T(8,128)(2,1)S(1)} %convolution_convert_fusion.7.q_ref, bf16[512,512]{1,0:T(8,128)(2,1)S(1)} %copy-done.19, bf16[512,512]{1,0:T(8,128)(2,1)S(1)} %get-tuple-element.122.kb_ref, bf16[512,512]{1,0:T(8,128)(2,1)S(1)} %copy-done.22, ...), custom_call_target="tpu_custom_call" | custom-call | flops 4294967296 | bytes 3145728 | tf_op jit(solution)/shard_map/pallas_call | solution.py:187
  121.9 3.2 collective-permute-done.9
  125.1 2.9 convert_add_fusion.4
  128.5 13.5 %maximum_maximum_fusion = bf16[1024,3072]{1,0:T(8,128)(2,1)} fusion(bf16[512,768]{1,0:T(8,128)(2,1)} %collective-permute-done.5, bf16[512,768]{1,0:T(8,128)(2,1)} %collective-permute-done.4, bf16[512,768]{1,0:T(8,128)(2,1)} %collective-permute-done.3, bf16[512,768]{1,0:T(8,128)(2,1)} %get-tuple-element.116, bf16[512,768]{1,0:T(8,128)(2,1)} %collective-permute-done.2, ...), kind=kLoop, calls=%fused_computation.2 | loop fusion | flops 50331648 | bytes 12582912 | tf_op jit(solution)/shard_map/concatenate | solution.py:272
  142.2 16.6 %collective-permute-done.10 = bf16[512,768]{1,0:T(8,128)(2,1)S(1)} collective-permute-done((bf16[512,768]{1,0:T(8,128)(2,1)S(1)}, bf16[512,768]{1,0:T(8,128)(2,1)S(1)}, u32[]{:S(2)}, u32[]{:S(2)}) %collective-permute-start.10) | collective-permute-done | bytes 786464 | tf_op jit(solution)/shard_map/ppermute | solution.py:25
  163.0 5.7 %psum.14 = f32[2,257]{1,0:T(2,128)S(1)} all-reduce(f32[2,257]{1,0:T(2,128)S(1)} %pad_maximum_fusion.18), channel_id=1, replica_groups=mesh['tm'=8,'tensor'=4] {'tensor'}, use_global_device_ids=true, to_apply=%region_2.3 | all-reduce | flops 514 | bytes 4112 | tf_op jit(solution)/shard_map/psum | solution.py:278
  171.7 5.4 %all_gather.7 = f32[2,3072]{1,0:T(2,128)S(1)} all-gather(f32[2,768]{1,0:T(2,128)S(1)} %get-tuple-element.124), channel_id=1, replica_groups=mesh['tm'=8,'tensor'=4] {'tensor'}, dimensions={1}, use_global_device_ids=true | all-gather | bytes 30720 | tf_op jit(solution)/shard_map/all_gather | solution.py:309
  178.8 4.5 fusion
  183.3 3.7 convolution_convert_fusion.3
  187.1 3.4 convolution_convert_fusion.6
  190.7 9.8 %shard_map.180 = (bf16[512,512]{1,0:T(8,128)(2,1)S(1)}, bf16[512,512]{1,0:T(8,128)(2,1)S(1)}, bf16[512,512]{1,0:T(8,128)(2,1)S(1)}, bf16[512,512]{1,0:T(8,128)(2,1)S(1)}, bf16[512,512]{1,0:T(8,128)(2,1)S(1)}) custom-call(s32[1]{0:T(128)} %bitcast.cut_ref, bf16[512,512]{1,0:T(8,128)(2,1)S(1)} %copy-done.25, bf16[512,512]{1,0:T(8,128)(2,1)S(1)} %copy-done.20, ...), custom_call_target="tpu_custom_call" | custom-call | flops 10737418240 | bytes 5767168 | tf_op jit(solution)/shard_map/pallas_call | solution.py:187
  202.3 5.3 %collective-permute-start.12 = (bf16[512,1024]{1,0:T(8,128)(2,1)}, bf16[512,1024]{1,0:T(8,128)(2,1)}, u32[]{:S(2)}, u32[]{:S(2)}) collective-permute-start(bf16[512,1024]{1,0:T(8,128)(2,1)} %constant_dynamic-update-slice_fusion), channel_id=1, source_target_pairs={{0,4},{4,8},{8,12},{12,16},{16,20},{20,24},{24,28},{1,5},{5,9},{9,... | collective-permute-start | bytes 3145736 | tf_op jit(solution)/shard_map/ppermute | solution.py:21
  207.6 9.8 %shard_map.181 = (bf16[512,512]{1,0:T(8,128)(2,1)S(1)}, bf16[512,512]{1,0:T(8,128)(2,1)S(1)}, bf16[512,512]{1,0:T(8,128)(2,1)S(1)}, bf16[512,512]{1,0:T(8,128)(2,1)S(1)}, bf16[512,512]{1,0:T(8,128)(2,1)S(1)}) custom-call(s32[1]{0:T(128)} %constant.176.clone.1.cut_ref, bf16[512,512]{1,0:T(8,128)(2,1)S(1)} %copy-done.17, bf16[512,512]{1,0:T(8,128)(2,1)S(1)} %copy-done.4, ...), custom_call_target="tpu_custom_call" | custom-call | flops 10737418240 | bytes 5767168 | tf_op jit(solution)/shard_map/pallas_call | solution.py:187
  217.5 3.8 convolution_convert_fusion.2
  224.7 2.6 copy.38
  229.3 2.6 copy.45
  233.9 6.8 %convolution_convert_fusion = bf16[3072,512]{1,0:T(8,128)(2,1)S(1)} fusion(bf16[1024,3072]{1,0:T(8,128)(2,1)} %maximum_maximum_fusion, bf16[512,512]{1,0:T(8,128)(2,1)S(1)} %add_convert_fusion.2, bf16[512,512]{1,0:T(8,128)(2,1)S(1)} %get-tuple-element.117), kind=kOutput, calls=%fused_computation.3 | convolution fusion | flops 3224895488 | bytes 10485760 | tf_op jit(solution)/shard_map/dot_general | solution.py:15
  243.4 3.8 convolution_convert_fusion.1
  249.5 16.8 %collective-permute-done.11 = bf16[4,384,512]{2,1,0:T(8,128)(2,1)} collective-permute-done((bf16[4,384,512]{2,1,0:T(8,128)(2,1)}, bf16[4,384,512]{2,1,0:T(8,128)(2,1)}, u32[]{:S(2)}, u32[]{:S(2)}) %collective-permute-start.11) | collective-permute-done | bytes 1572896 | tf_op jit(solution)/shard_map/ppermute | solution.py:25
  268.3 4.7 %collective-permute-start.13 = (bf16[384,512]{1,0:T(8,128)(2,1)S(1)}, bf16[384,512]{1,0:T(8,128)(2,1)S(1)}, u32[]{:S(2)}, u32[]{:S(2)}) collective-permute-start(bf16[384,512]{1,0:T(8,128)(2,1)S(1)} %get-tuple-element.111), channel_id=1, source_target_pairs={{0,8},{4,12},{1,9},{5,13},{2,10},{6,14},{3,11},{7,15}} | collective-permute-start | bytes 1179656 | tf_op jit(solution)/shard_map/ppermute | solution.py:127
  273.0 27.0 %collective-permute-done.33 = bf16[4,384,512]{1,2,0:T(8,128)(2,1)} collective-permute-done((bf16[4,384,512]{1,2,0:T(8,128)(2,1)}, bf16[4,384,512]{1,2,0:T(8,128)(2,1)}, u32[]{:S(2)}, u32[]{:S(2)}) %collective-permute-start.33) | collective-permute-done | bytes 1572896 | tf_op jit(solution)/shard_map/ppermute | solution.py:25
  302.7 4.7 %collective-permute-start.34 = (bf16[384,512]{0,1:T(8,128)(2,1)S(1)}, bf16[384,512]{0,1:T(8,128)(2,1)S(1)}, u32[]{:S(2)}, u32[]{:S(2)}) collective-permute-start(bf16[384,512]{0,1:T(8,128)(2,1)S(1)} %get-tuple-element.99), channel_id=1, source_target_pairs={{0,8},{4,12},{1,9},{5,13},{2,10},{6,14},{3,11},{7,15}} | collective-permute-start | bytes 1179656 | tf_op jit(solution)/shard_map/ppermute | solution.py:127
  311.7 4.2 collective-permute-done.34
  315.9 5.1 %collective-permute-start.14 = (bf16[384,512]{1,0:T(8,128)(2,1)}, bf16[384,512]{1,0:T(8,128)(2,1)}, u32[]{:S(2)}, u32[]{:S(2)}) collective-permute-start(bf16[384,512]{1,0:T(8,128)(2,1)} %fusion.36), channel_id=1, source_target_pairs={{0,8},{4,12},{8,16},{12,20},{1,9},{5,13},{9,17},{13,21},{2,10},{6,... | collective-permute-start | bytes 1179656 | tf_op jit(solution)/shard_map/ppermute | solution.py:127
  332.7 4.4 collective-permute-start.15
  342.8 5.1 %collective-permute-start.20 = (bf16[384,512]{1,0:T(8,128)(2,1)S(1)}, bf16[384,512]{1,0:T(8,128)(2,1)S(1)}, u32[]{:S(2)}, u32[]{:S(2)}) collective-permute-start(bf16[384,512]{1,0:T(8,128)(2,1)S(1)} %get-tuple-element.107), channel_id=1, source_target_pairs={{0,8},{4,12},{1,9},{5,13},{2,10},{6,14},{3,11},{7,15}} | collective-permute-start | bytes 1179656 | tf_op jit(solution)/shard_map/ppermute | solution.py:127
  347.8 19.0 %collective-permute-done.26 = bf16[4,384,512]{2,1,0:T(8,128)(2,1)} collective-permute-done((bf16[4,384,512]{2,1,0:T(8,128)(2,1)}, bf16[4,384,512]{2,1,0:T(8,128)(2,1)}, u32[]{:S(2)}, u32[]{:S(2)}) %collective-permute-start.26) | collective-permute-done | bytes 1572896 | tf_op jit(solution)/shard_map/ppermute | solution.py:25
  369.5 5.3 %collective-permute-start.27 = (bf16[384,512]{1,0:T(8,128)(2,1)S(1)}, bf16[384,512]{1,0:T(8,128)(2,1)S(1)}, u32[]{:S(2)}, u32[]{:S(2)}) collective-permute-start(bf16[384,512]{1,0:T(8,128)(2,1)S(1)} %get-tuple-element.103), channel_id=1, source_target_pairs={{0,8},{4,12},{1,9},{5,13},{2,10},{6,14},{3,11},{7,15}} | collective-permute-start | bytes 1179656 | tf_op jit(solution)/shard_map/ppermute | solution.py:127
  375.7 7.6 %collective-permute-done.27 = bf16[384,512]{1,0:T(8,128)(2,1)S(1)} collective-permute-done((bf16[384,512]{1,0:T(8,128)(2,1)S(1)}, bf16[384,512]{1,0:T(8,128)(2,1)S(1)}, u32[]{:S(2)}, u32[]{:S(2)}) %collective-permute-start.27) | collective-permute-done | bytes 393248 | tf_op jit(solution)/shard_map/ppermute | solution.py:127
  383.3 4.4 collective-permute-start.21
  391.9 5.4 %collective-permute-done.21 = bf16[384,512]{1,0:T(8,128)(2,1)S(1)} collective-permute-done((bf16[384,512]{1,0:T(8,128)(2,1)S(1)}, bf16[384,512]{1,0:T(8,128)(2,1)S(1)}, u32[]{:S(2)}, u32[]{:S(2)}) %collective-permute-start.21) | collective-permute-done | bytes 393248 | tf_op jit(solution)/shard_map/ppermute | solution.py:127
  400.1 5.6 %collective-permute-done.28 = bf16[384,512]{1,0:T(8,128)(2,1)S(1)} collective-permute-done((bf16[384,512]{1,0:T(8,128)(2,1)S(1)}, bf16[384,512]{1,0:T(8,128)(2,1)S(1)}, u32[]{:S(2)}, u32[]{:S(2)}) %collective-permute-start.28) | collective-permute-done | bytes 393248 | tf_op jit(solution)/shard_map/ppermute | solution.py:127
  406.6 5.7 %collective-permute-done.36 = bf16[384,512]{0,1:T(8,128)(2,1)S(1)} collective-permute-done((bf16[384,512]{0,1:T(8,128)(2,1)S(1)}, bf16[384,512]{0,1:T(8,128)(2,1)S(1)}, u32[]{:S(2)}, u32[]{:S(2)}) %collective-permute-start.36) | collective-permute-done | bytes 393248 | tf_op jit(solution)/shard_map/ppermute | solution.py:127
  414.0 5.0 %collective-permute-start.22 = (bf16[384,512]{1,0:T(8,128)(2,1)S(1)}, bf16[384,512]{1,0:T(8,128)(2,1)S(1)}, u32[]{:S(2)}, u32[]{:S(2)}) collective-permute-start(bf16[384,512]{1,0:T(8,128)(2,1)S(1)} %get-tuple-element.105), channel_id=1, source_target_pairs={{0,8},{4,12},{8,16},{12,20},{16,24},{20,28},{1,9},{5,13},{9,17},{1... | collective-permute-start | bytes 1179656 | tf_op jit(solution)/shard_map/ppermute | solution.py:127
  419.0 13.1 %collective-permute-start.29 = (bf16[384,512]{1,0:T(8,128)(2,1)S(1)}, bf16[384,512]{1,0:T(8,128)(2,1)S(1)}, u32[]{:S(2)}, u32[]{:S(2)}) collective-permute-start(bf16[384,512]{1,0:T(8,128)(2,1)S(1)} %get-tuple-element.101), channel_id=1, source_target_pairs={{0,8},{4,12},{8,16},{12,20},{16,24},{20,28},{1,9},{5,13},{9,17},{1... | collective-permute-start | bytes 1179656 | tf_op jit(solution)/shard_map/ppermute | solution.py:127
  437.3 8.0 %collective-permute-done.25 = bf16[384,512]{1,0:T(8,128)(2,1)S(1)} collective-permute-done((bf16[384,512]{1,0:T(8,128)(2,1)S(1)}, bf16[384,512]{1,0:T(8,128)(2,1)S(1)}, u32[]{:S(2)}, u32[]{:S(2)}) %collective-permute-start.25) | collective-permute-done | bytes 393248 | tf_op jit(solution)/shard_map/ppermute | solution.py:130
  446.4 3.2 collective-permute-done.32
  (293 shorter events, 97.2 us)
Async XLA Ops:
  8.0 63.7 %copy-start = (bf16[512,3072]{1,0:T(8,128)(2,1)S(1)}, bf16[512,3072]{1,0:T(8,128)(2,1)}, u32[]{:S(2)}) copy-start(bf16[512,3072]{1,0:T(8,128)(2,1)} %param.15) | copy-start | bytes 9437188
  8.0 170.8 %all-gather.2.cloned.1.call-start = ((), (), s32[]{:S(2)}) async-start(), calls=%async_computation | async-start | bytes 7864320 | tf_op jit(solution)/shard_map/all_gather | solution.py:250
  10.8 20.8 %collective-permute-start.1 = (bf16[512,768]{1,0:T(8,128)(2,1)}, bf16[512,768]{1,0:T(8,128)(2,1)}, u32[]{:S(2)}, u32[]{:S(2)}) collective-permute-start(bf16[512,768]{1,0:T(8,128)(2,1)} %get-tuple-element.115), channel_id=1, source_target_pairs={{0,2},{1,3},{2,0},{3,1},{4,6},{5,7},{6,4},{7,5},{8,10},{9,11},{10,... | collective-permute-start | bytes 2359304 | tf_op jit(solution)/shard_map/ppermute | solution.py:25
  13.8 24.2 %collective-permute-start = (bf16[512,768]{1,0:T(8,128)(2,1)}, bf16[512,768]{1,0:T(8,128)(2,1)}, u32[]{:S(2)}, u32[]{:S(2)}) collective-permute-start(bf16[512,768]{1,0:T(8,128)(2,1)} %get-tuple-element.115), channel_id=1, source_target_pairs={{0,1},{1,0},{2,3},{3,2},{4,5},{5,4},{6,7},{7,6},{8,9},{9,8},{10,11... | collective-permute-start | bytes 2359304 | tf_op jit(solution)/shard_map/ppermute | solution.py:25
  31.7 6.4 %collective-permute-start.2 = (bf16[512,768]{1,0:T(8,128)(2,1)}, bf16[512,768]{1,0:T(8,128)(2,1)}, u32[]{:S(2)}, u32[]{:S(2)}) collective-permute-start(bf16[512,768]{1,0:T(8,128)(2,1)} %collective-permute-done.1), channel_id=1, source_target_pairs={{0,1},{1,0},{2,3},{3,2},{4,5},{5,4},{6,7},{7,6},{8,9},{9,8},{10,11... | collective-permute-start | bytes 2359304 | tf_op jit(solution)/shard_map/ppermute | solution.py:25
  31.7 21.8 %collective-permute-start.4 = (bf16[512,768]{1,0:T(8,128)(2,1)}, bf16[512,768]{1,0:T(8,128)(2,1)}, u32[]{:S(2)}, u32[]{:S(2)}) collective-permute-start(bf16[512,768]{1,0:T(8,128)(2,1)} %get-tuple-element.116), channel_id=1, source_target_pairs={{0,2},{1,3},{2,0},{3,1},{4,6},{5,7},{6,4},{7,5},{8,10},{9,11},{10,... | collective-permute-start | bytes 2359304 | tf_op jit(solution)/shard_map/ppermute | solution.py:25
  33.4 20.4 %collective-permute-start.3 = (bf16[512,768]{1,0:T(8,128)(2,1)}, bf16[512,768]{1,0:T(8,128)(2,1)}, u32[]{:S(2)}, u32[]{:S(2)}) collective-permute-start(bf16[512,768]{1,0:T(8,128)(2,1)} %get-tuple-element.116), channel_id=1, source_target_pairs={{0,1},{1,0},{2,3},{3,2},{4,5},{5,4},{6,7},{7,6},{8,9},{9,8},{10,11... | collective-permute-start | bytes 2359304 | tf_op jit(solution)/shard_map/ppermute | solution.py:25
  53.5 2.6 collective-permute-start.5
  76.2 29.1 %collective-permute-start.6 = (bf16[1024,768]{1,0:T(8,128)(2,1)}, bf16[1024,768]{1,0:T(8,128)(2,1)}, u32[]{:S(2)}, u32[]{:S(2)}) collective-permute-start(bf16[1024,768]{1,0:T(8,128)(2,1)} %broadcast_select_fusion.1), channel_id=1, source_target_pairs={{0,1},{1,0},{2,3},{3,2},{4,5},{5,4},{6,7},{7,6},{8,9},{9,8},{10,11... | collective-permute-start | bytes 4718600 | tf_op jit(solution)/shard_map/ppermute | solution.py:25
  76.5 27.5 %collective-permute-start.8 = (bf16[512,1024]{1,0:T(8,128)(2,1)}, bf16[512,1024]{1,0:T(8,128)(2,1)}, u32[]{:S(2)}, u32[]{:S(2)}) collective-permute-start(bf16[512,1024]{1,0:T(8,128)(2,1)} %pad_maximum_fusion.10), channel_id=1, source_target_pairs={{4,0},{8,4},{12,8},{16,12},{20,16},{24,20},{28,24},{5,1},{9,5},{13... | collective-permute-start | bytes 3145736 | tf_op jit(solution)/shard_map/ppermute | solution.py:21
  77.8 247.7 %all-reduce.2.cloned.1.call-start = ((), (), s32[]{:S(2)}) async-start(), calls=%async_computation.1 | async-start | bytes 811008 | tf_op jit(solution)/shard_map/psum | solution.py:339
  121.2 3.8 collective-permute-start.9
  121.5 20.7 %collective-permute-start.7 = (bf16[512,768]{1,0:T(8,128)(2,1)}, bf16[512,768]{1,0:T(8,128)(2,1)S(1)}, u32[]{:S(2)}, u32[]{:S(2)}) collective-permute-start(bf16[512,768]{1,0:T(8,128)(2,1)} %select_convert_fusion.1), channel_id=1, source_target_pairs={{0,2},{1,3},{2,0},{3,1},{4,6},{5,7},{6,4},{7,5},{8,10},{9,11},{10,... | collective-permute-start | bytes 2359304 | tf_op jit(solution)/shard_map/ppermute | solution.py:25
  128.1 30.7 %copy-start.27 = (f32[1024,768]{1,0:T(8,128)S(1)}, f32[1024,768]{1,0:T(8,128)}, u32[]{:S(2)}) copy-start(f32[1024,768]{1,0:T(8,128)} %copy-done.26) | copy-start | bytes 9437188
  128.1 30.7 %copy-start.42 = (bf16[1024,768]{1,0:T(8,128)(2,1)S(1)}, bf16[1024,768]{1,0:T(8,128)(2,1)}, u32[]{:S(2)}) copy-start(bf16[1024,768]{1,0:T(8,128)(2,1)} %param.11) | copy-start | bytes 4718596
  128.1 30.6 %collective-permute-start.10 = (bf16[512,768]{1,0:T(8,128)(2,1)S(1)}, bf16[512,768]{1,0:T(8,128)(2,1)S(1)}, u32[]{:S(2)}, u32[]{:S(2)}) collective-permute-start(bf16[512,768]{1,0:T(8,128)(2,1)S(1)} %select_convert_fusion), channel_id=1, source_target_pairs={{0,2},{1,3},{2,0},{3,1},{4,6},{5,7},{6,4},{7,5},{8,10},{9,11},{10,... | collective-permute-start | bytes 2359304 | tf_op jit(solution)/shard_map/ppermute | solution.py:25
  202.3 29.9 %collective-permute-start.12 = (bf16[512,1024]{1,0:T(8,128)(2,1)}, bf16[512,1024]{1,0:T(8,128)(2,1)}, u32[]{:S(2)}, u32[]{:S(2)}) collective-permute-start(bf16[512,1024]{1,0:T(8,128)(2,1)} %constant_dynamic-update-slice_fusion), channel_id=1, source_target_pairs={{0,4},{4,8},{8,12},{12,16},{16,20},{20,24},{24,28},{1,5},{5,9},{9,... | collective-permute-start | bytes 3145736 | tf_op jit(solution)/shard_map/ppermute | solution.py:21
  222.6 43.7 %collective-permute-start.11 = (bf16[4,384,512]{2,1,0:T(8,128)(2,1)}, bf16[4,384,512]{2,1,0:T(8,128)(2,1)}, u32[]{:S(2)}, u32[]{:S(2)}) collective-permute-start(bf16[4,384,512]{2,1,0:T(8,128)(2,1)} %dynamic-slice_bitcast_fusion.2), channel_id=1, source_target_pairs={{0,4},{4,0},{8,12},{12,8},{16,20},{20,16},{24,28},{28,24},{1,5},{5... | collective-permute-start | bytes 4718600 | tf_op jit(solution)/shard_map/ppermute | solution.py:25
  227.3 72.8 %collective-permute-start.33 = (bf16[4,384,512]{1,2,0:T(8,128)(2,1)}, bf16[4,384,512]{1,2,0:T(8,128)(2,1)}, u32[]{:S(2)}, u32[]{:S(2)}) collective-permute-start(bf16[4,384,512]{1,2,0:T(8,128)(2,1)} %bitcast.154), channel_id=1, source_target_pairs={{0,4},{4,0},{8,12},{12,8},{16,20},{20,16},{24,28},{28,24},{1,5},{5... | collective-permute-start | bytes 4718600 | tf_op jit(solution)/shard_map/ppermute | solution.py:25
  242.0 98.7 %collective-permute-start.19 = (bf16[4,384,512]{2,1,0:T(8,128)(2,1)}, bf16[4,384,512]{2,1,0:T(8,128)(2,1)}, u32[]{:S(2)}, u32[]{:S(2)}) collective-permute-start(bf16[4,384,512]{2,1,0:T(8,128)(2,1)} %dynamic-slice_bitcast_fusion), channel_id=1, source_target_pairs={{0,4},{4,0},{8,12},{12,8},{16,20},{20,16},{24,28},{28,24},{1,5},{5... | collective-permute-start | bytes 4718600 | tf_op jit(solution)/shard_map/ppermute | solution.py:25
  249.5 50.5 %copy-start.41 = (bf16[4,1,384,512]{2,3,0,1:T(8,128)(2,1)S(1)}, bf16[4,1,384,512]{2,3,0,1:T(8,128)(2,1)}, u32[]{:S(2)}) copy-start(bf16[4,1,384,512]{2,3,0,1:T(8,128)(2,1)} %copy.45) | copy-start | bytes 4718596
  268.2 121.6 %copy-start.28 = (bf16[4,384,512]{2,1,0:T(8,128)(2,1)}, bf16[4,384,512]{2,1,0:T(8,128)(2,1)S(1)}, u32[]{:S(2)}) copy-start(bf16[4,384,512]{2,1,0:T(8,128)(2,1)S(1)} %fusion.4) | copy-start | bytes 4718596
  268.3 41.1 %collective-permute-start.13 = (bf16[384,512]{1,0:T(8,128)(2,1)S(1)}, bf16[384,512]{1,0:T(8,128)(2,1)S(1)}, u32[]{:S(2)}, u32[]{:S(2)}) collective-permute-start(bf16[384,512]{1,0:T(8,128)(2,1)S(1)} %get-tuple-element.111), channel_id=1, source_target_pairs={{0,8},{4,12},{1,9},{5,13},{2,10},{6,14},{3,11},{7,15}} | collective-permute-start | bytes 1179656 | tf_op jit(solution)/shard_map/ppermute | solution.py:127
  302.7 13.2 %collective-permute-start.34 = (bf16[384,512]{0,1:T(8,128)(2,1)S(1)}, bf16[384,512]{0,1:T(8,128)(2,1)S(1)}, u32[]{:S(2)}, u32[]{:S(2)}) collective-permute-start(bf16[384,512]{0,1:T(8,128)(2,1)S(1)} %get-tuple-element.99), channel_id=1, source_target_pairs={{0,8},{4,12},{1,9},{5,13},{2,10},{6,14},{3,11},{7,15}} | collective-permute-start | bytes 1179656 | tf_op jit(solution)/shard_map/ppermute | solution.py:127
  307.4 59.4 %collective-permute-start.26 = (bf16[4,384,512]{2,1,0:T(8,128)(2,1)}, bf16[4,384,512]{2,1,0:T(8,128)(2,1)}, u32[]{:S(2)}, u32[]{:S(2)}) collective-permute-start(bf16[4,384,512]{2,1,0:T(8,128)(2,1)} %dynamic-slice_bitcast_fusion.1), channel_id=1, source_target_pairs={{0,4},{4,0},{8,12},{12,8},{16,20},{20,16},{24,28},{28,24},{1,5},{5... | collective-permute-start | bytes 4718600 | tf_op jit(solution)/shard_map/ppermute | solution.py:25
  308.7 13.1 %collective-permute-start.16 = (bf16[384,512]{1,0:T(8,128)(2,1)S(1)}, bf16[384,512]{1,0:T(8,128)(2,1)S(1)}, u32[]{:S(2)}, u32[]{:S(2)}) collective-permute-start(bf16[384,512]{1,0:T(8,128)(2,1)S(1)} %get-tuple-element.112), channel_id=1, source_target_pairs={{24,16},{28,20},{25,17},{29,21},{26,18},{30,22},{27,19},{31,23}} | collective-permute-start | bytes 1179656 | tf_op jit(solution)/shard_map/ppermute | solution.py:130
  309.4 23.3 %collective-permute-start.37 = (bf16[384,512]{0,1:T(8,128)(2,1)}, bf16[384,512]{0,1:T(8,128)(2,1)}, u32[]{:S(2)}, u32[]{:S(2)}) collective-permute-start(bf16[384,512]{0,1:T(8,128)(2,1)} %get-tuple-element.100), channel_id=1, source_target_pairs={{24,16},{28,20},{25,17},{29,21},{26,18},{30,22},{27,19},{31,23}} | collective-permute-start | bytes 1179656 | tf_op jit(solution)/shard_map/ppermute | solution.py:130
  315.9 14.5 %collective-permute-start.14 = (bf16[384,512]{1,0:T(8,128)(2,1)}, bf16[384,512]{1,0:T(8,128)(2,1)}, u32[]{:S(2)}, u32[]{:S(2)}) collective-permute-start(bf16[384,512]{1,0:T(8,128)(2,1)} %fusion.36), channel_id=1, source_target_pairs={{0,8},{4,12},{8,16},{12,20},{1,9},{5,13},{9,17},{13,21},{2,10},{6,... | collective-permute-start | bytes 1179656 | tf_op jit(solution)/shard_map/ppermute | solution.py:127
  322.6 15.9 %collective-permute-start.35 = (bf16[384,512]{0,1:T(8,128)(2,1)}, bf16[384,512]{0,1:T(8,128)(2,1)}, u32[]{:S(2)}, u32[]{:S(2)}) collective-permute-start(bf16[384,512]{0,1:T(8,128)(2,1)} %fusion.20), channel_id=1, source_target_pairs={{0,8},{4,12},{8,16},{12,20},{1,9},{5,13},{9,17},{13,21},{2,10},{6,... | collective-permute-start | bytes 1179656 | tf_op jit(solution)/shard_map/ppermute | solution.py:127
  332.0 55.8 %collective-permute-start.17 = (bf16[384,512]{1,0:T(8,128)(2,1)S(1)}, bf16[384,512]{1,0:T(8,128)(2,1)S(1)}, u32[]{:S(2)}, u32[]{:S(2)}) collective-permute-start(bf16[384,512]{1,0:T(8,128)(2,1)S(1)} %get-tuple-element.110), channel_id=1, source_target_pairs={{24,16},{28,20},{16,8},{20,12},{25,17},{29,21},{17,9},{21,13},{26,... | collective-permute-start | bytes 1179656 | tf_op jit(solution)/shard_map/ppermute | solution.py:130
  332.7 100.9 %collective-permute-start.15 = (bf16[384,512]{1,0:T(8,128)(2,1)S(1)}, bf16[384,512]{1,0:T(8,128)(2,1)S(1)}, u32[]{:S(2)}, u32[]{:S(2)}) collective-permute-start(bf16[384,512]{1,0:T(8,128)(2,1)S(1)} %get-tuple-element.109), channel_id=1, source_target_pairs={{0,8},{4,12},{8,16},{12,20},{16,24},{20,28},{1,9},{5,13},{9,17},{1... | collective-permute-start | bytes 1179656 | tf_op jit(solution)/shard_map/ppermute | solution.py:127
  339.9 27.6 %copy-start.45 = (bf16[3072,512]{1,0:T(8,128)(2,1)S(1)}, bf16[3072,512]{1,0:T(8,128)(2,1)}, u32[]{:S(2)}) copy-start(bf16[3072,512]{1,0:T(8,128)(2,1)} %copy-done.44) | copy-start | bytes 9437188
  339.9 29.6 %collective-permute-start.38 = (bf16[384,512]{0,1:T(8,128)(2,1)S(1)}, bf16[384,512]{0,1:T(8,128)(2,1)S(1)}, u32[]{:S(2)}, u32[]{:S(2)}) collective-permute-start(bf16[384,512]{0,1:T(8,128)(2,1)S(1)} %get-tuple-element.98), channel_id=1, source_target_pairs={{24,16},{28,20},{16,8},{20,12},{25,17},{29,21},{17,9},{21,13},{26,... | collective-permute-start | bytes 1179656 | tf_op jit(solution)/shard_map/ppermute | solution.py:130
  342.8 32.1 %collective-permute-start.20 = (bf16[384,512]{1,0:T(8,128)(2,1)S(1)}, bf16[384,512]{1,0:T(8,128)(2,1)S(1)}, u32[]{:S(2)}, u32[]{:S(2)}) collective-permute-start(bf16[384,512]{1,0:T(8,128)(2,1)S(1)} %get-tuple-element.107), channel_id=1, source_target_pairs={{0,8},{4,12},{1,9},{5,13},{2,10},{6,14},{3,11},{7,15}} | collective-permute-start | bytes 1179656 | tf_op jit(solution)/shard_map/ppermute | solution.py:127
  366.9 23.1 %collective-permute-start.23 = (bf16[384,512]{1,0:T(8,128)(2,1)S(1)}, bf16[384,512]{1,0:T(8,128)(2,1)S(1)}, u32[]{:S(2)}, u32[]{:S(2)}) collective-permute-start(bf16[384,512]{1,0:T(8,128)(2,1)S(1)} %get-tuple-element.108), channel_id=1, source_target_pairs={{24,16},{28,20},{25,17},{29,21},{26,18},{30,22},{27,19},{31,23}} | collective-permute-start | bytes 1179656 | tf_op jit(solution)/shard_map/ppermute | solution.py:130
  369.5 13.8 %collective-permute-start.27 = (bf16[384,512]{1,0:T(8,128)(2,1)S(1)}, bf16[384,512]{1,0:T(8,128)(2,1)S(1)}, u32[]{:S(2)}, u32[]{:S(2)}) collective-permute-start(bf16[384,512]{1,0:T(8,128)(2,1)S(1)} %get-tuple-element.103), channel_id=1, source_target_pairs={{0,8},{4,12},{1,9},{5,13},{2,10},{6,14},{3,11},{7,15}} | collective-permute-start | bytes 1179656 | tf_op jit(solution)/shard_map/ppermute | solution.py:127
  374.9 23.9 %collective-permute-start.30 = (bf16[384,512]{1,0:T(8,128)(2,1)S(1)}, bf16[384,512]{1,0:T(8,128)(2,1)S(1)}, u32[]{:S(2)}, u32[]{:S(2)}) collective-permute-start(bf16[384,512]{1,0:T(8,128)(2,1)S(1)} %get-tuple-element.104), channel_id=1, source_target_pairs={{24,16},{28,20},{25,17},{29,21},{26,18},{30,22},{27,19},{31,23}} | collective-permute-start | bytes 1179656 | tf_op jit(solution)/shard_map/ppermute | solution.py:130
  383.3 13.9 %collective-permute-start.21 = (bf16[384,512]{1,0:T(8,128)(2,1)S(1)}, bf16[384,512]{1,0:T(8,128)(2,1)S(1)}, u32[]{:S(2)}, u32[]{:S(2)}) collective-permute-start(bf16[384,512]{1,0:T(8,128)(2,1)S(1)} %fusion.31), channel_id=1, source_target_pairs={{0,8},{4,12},{8,16},{12,20},{1,9},{5,13},{9,17},{13,21},{2,10},{6,... | collective-permute-start | bytes 1179656 | tf_op jit(solution)/shard_map/ppermute | solution.py:127
  387.9 17.8 %collective-permute-start.28 = (bf16[384,512]{1,0:T(8,128)(2,1)S(1)}, bf16[384,512]{1,0:T(8,128)(2,1)S(1)}, u32[]{:S(2)}, u32[]{:S(2)}) collective-permute-start(bf16[384,512]{1,0:T(8,128)(2,1)S(1)} %fusion.26), channel_id=1, source_target_pairs={{0,8},{4,12},{8,16},{12,20},{1,9},{5,13},{9,17},{13,21},{2,10},{6,... | collective-permute-start | bytes 1179656 | tf_op jit(solution)/shard_map/ppermute | solution.py:127
  389.9 22.4 %collective-permute-start.36 = (bf16[384,512]{0,1:T(8,128)(2,1)S(1)}, bf16[384,512]{0,1:T(8,128)(2,1)S(1)}, u32[]{:S(2)}, u32[]{:S(2)}) collective-permute-start(bf16[384,512]{0,1:T(8,128)(2,1)S(1)} %get-tuple-element.97), channel_id=1, source_target_pairs={{0,8},{4,12},{8,16},{12,20},{16,24},{20,28},{1,9},{5,13},{9,17},{1... | collective-permute-start | bytes 1179656 | tf_op jit(solution)/shard_map/ppermute | solution.py:127
  397.3 15.7 %collective-permute-start.39 = (bf16[384,512]{0,1:T(8,128)(2,1)S(1)}, bf16[384,512]{0,1:T(8,128)(2,1)S(1)}, u32[]{:S(2)}, u32[]{:S(2)}) collective-permute-start(bf16[384,512]{0,1:T(8,128)(2,1)S(1)} %fusion.19), channel_id=1, source_target_pairs={{24,16},{28,20},{16,8},{20,12},{8,0},{12,4},{25,17},{29,21},{17,9}... | collective-permute-start | bytes 1179656 | tf_op jit(solution)/shard_map/ppermute | solution.py:130
  398.8 36.5 %collective-permute-start.18 = (bf16[384,512]{1,0:T(8,128)(2,1)S(1)}, bf16[384,512]{1,0:T(8,128)(2,1)S(1)}, u32[]{:S(2)}, u32[]{:S(2)}) collective-permute-start(bf16[384,512]{1,0:T(8,128)(2,1)S(1)} %fusion.35), channel_id=1, source_target_pairs={{24,16},{28,20},{16,8},{20,12},{8,0},{12,4},{25,17},{29,21},{17,9}... | collective-permute-start | bytes 1179656 | tf_op jit(solution)/shard_map/ppermute | solution.py:130
  405.7 13.3 %collective-permute-start.24 = (bf16[384,512]{1,0:T(8,128)(2,1)S(1)}, bf16[384,512]{1,0:T(8,128)(2,1)S(1)}, u32[]{:S(2)}, u32[]{:S(2)}) collective-permute-start(bf16[384,512]{1,0:T(8,128)(2,1)S(1)} %get-tuple-element.106), channel_id=1, source_target_pairs={{24,16},{28,20},{16,8},{20,12},{25,17},{29,21},{17,9},{21,13},{26,... | collective-permute-start | bytes 1179656 | tf_op jit(solution)/shard_map/ppermute | solution.py:130
  412.3 19.9 %collective-permute-start.31 = (bf16[384,512]{1,0:T(8,128)(2,1)S(1)}, bf16[384,512]{1,0:T(8,128)(2,1)S(1)}, u32[]{:S(2)}, u32[]{:S(2)}) collective-permute-start(bf16[384,512]{1,0:T(8,128)(2,1)S(1)} %get-tuple-element.102), channel_id=1, source_target_pairs={{24,16},{28,20},{16,8},{20,12},{25,17},{29,21},{17,9},{21,13},{26,... | collective-permute-start | bytes 1179656 | tf_op jit(solution)/shard_map/ppermute | solution.py:130
  414.0 23.3 %collective-permute-start.22 = (bf16[384,512]{1,0:T(8,128)(2,1)S(1)}, bf16[384,512]{1,0:T(8,128)(2,1)S(1)}, u32[]{:S(2)}, u32[]{:S(2)}) collective-permute-start(bf16[384,512]{1,0:T(8,128)(2,1)S(1)} %get-tuple-element.105), channel_id=1, source_target_pairs={{0,8},{4,12},{8,16},{12,20},{16,24},{20,28},{1,9},{5,13},{9,17},{1... | collective-permute-start | bytes 1179656 | tf_op jit(solution)/shard_map/ppermute | solution.py:127
  419.0 27.3 %collective-permute-start.29 = (bf16[384,512]{1,0:T(8,128)(2,1)S(1)}, bf16[384,512]{1,0:T(8,128)(2,1)S(1)}, u32[]{:S(2)}, u32[]{:S(2)}) collective-permute-start(bf16[384,512]{1,0:T(8,128)(2,1)S(1)} %get-tuple-element.101), channel_id=1, source_target_pairs={{0,8},{4,12},{8,16},{12,20},{16,24},{20,28},{1,9},{5,13},{9,17},{1... | collective-permute-start | bytes 1179656 | tf_op jit(solution)/shard_map/ppermute | solution.py:127
  432.2 13.1 %collective-permute-start.25 = (bf16[384,512]{1,0:T(8,128)(2,1)S(1)}, bf16[384,512]{1,0:T(8,128)(2,1)S(1)}, u32[]{:S(2)}, u32[]{:S(2)}) collective-permute-start(bf16[384,512]{1,0:T(8,128)(2,1)S(1)} %fusion.30), channel_id=1, source_target_pairs={{24,16},{28,20},{16,8},{20,12},{8,0},{12,4},{25,17},{29,21},{17,9}... | collective-permute-start | bytes 1179656 | tf_op jit(solution)/shard_map/ppermute | solution.py:130
  433.7 15.9 %collective-permute-start.32 = (bf16[384,512]{1,0:T(8,128)(2,1)S(1)}, bf16[384,512]{1,0:T(8,128)(2,1)S(1)}, u32[]{:S(2)}, u32[]{:S(2)}) collective-permute-start(bf16[384,512]{1,0:T(8,128)(2,1)S(1)} %fusion.25), channel_id=1, source_target_pairs={{24,16},{28,20},{16,8},{20,12},{8,0},{12,4},{25,17},{29,21},{17,9}... | collective-permute-start | bytes 1179656 | tf_op jit(solution)/shard_map/ppermute | solution.py:130
  (71 other events, 538.7 us)
Sparse Core Ops, SparseCore 0:
  77.9 49.0 all-gather.1
Sparse Core Ops, SparseCore 1:
  178.9 79.1 all-reduce.1
